TPU v7x, 32 devices: a whole 2x2x4 slice. The times are simulated.
32 devices in a mesh: grp: 2 (over y), col: 8 (over z, x), sub: 2 (over core).
Axes of the slice: x: 2, y: 2, z: 4, core: 2. Of those that a mesh axis runs over, the one named last changes fastest.
Arguments:
- features: bfloat16 [1024, 131072], P('col', 'grp'), parts along dimension 1, may hold values from -6 to 6
- block_nodes: int32 [16, 2, 32], P('grp', 'sub'), parts along dimension 0, may hold values from 0 to 65535
- hop_two: int32 [16, 2, 10, 32], P('grp', 'sub'), parts along dimension 0, may hold values from 0 to 65535
- hop_two_count: int32 [16, 2, 32], P('grp', 'sub'), parts along dimension 0, may hold values from 1 to 10
- hop_one: int32 [16, 2, 25, 1], P(('grp', 'col'), 'sub'), parts along dimension 0, may hold values from 0 to 31
- hop_one_count: int32 [16, 2, 1], P(('grp', 'col'), 'sub'), parts along dimension 0, may hold values from 1 to 25
- labels: int32 [16, 2, 1, 112], P(('grp', 'col'), 'sub'), parts along dimension 0, may hold values 0 or 1
- weight_one: bfloat16 [2, 1024, 256], P(None, 'col'), may hold values from -0.125 to 0.125
- weight_two: bfloat16 [2, 256, 256], replicated, may hold values from -0.25 to 0.25
- weight_three: bfloat16 [256, 112], replicated, may hold values from -0.375 to 0.375
Outputs:
- hidden_one: bfloat16 [16, 2, 32, 256], P(('grp', 'col'), 'sub'), parts along dimension 0
- batch_loss: float32 [16, 2], P(('grp', 'col'), 'sub'), parts along dimension 0
- grad_weight_one: float32 [4, 1024, 256], P('grp', 'col'), parts along dimension 0
- grad_weight_two: float32 [4, 256, 256], P('grp'), parts along dimension 0
- grad_weight_three: float32 [512, 112], P('grp'), parts along dimension 0
There are 2 independent parts, one for each index of `grp`. A program takes and returns all parts, laid end to end along the dimension named above; an argument that names none is the same for every part. Nothing has to cross between parts.
Inputs may be any that keep to these rules, and one draw needn't show every extreme that they name: `hop_one`: rows of the same batch's block.
All inputs are finite; a program needn't handle non-finite values. No bound on the sum of `labels` on one device may be relied on, other than what follows from the above.
Results may differ from a plain program's by a relative error of at most 0.007.
Values may be sent and summed in bfloat16 or wider, within the bound.
No kernel may reach another device: no remote copies, remote signals or barrier semaphores. Data moves between devices by JAX's collectives and lax.ppermute only.
A program may use at most 128 MiB of HBM per device.

v0:
```python
import jax
import jax.numpy as jnp
from jax import lax
from jax.sharding import PartitionSpec as P


def silu_slope(value):
    sig = jax.nn.sigmoid(value)
    return sig * (1.0 + value * (1.0 - sig))


def per_device(
    features,
    block_nodes,
    hop_two,
    hop_two_count,
    hop_one,
    hop_one_count,
    labels,
    weight_one,
    weight_two,
    weight_three,
):
    groups = lax.axis_size("col")
    feature_depth = weight_one.shape[1]
    width = weight_one.shape[2]
    block_rows = block_nodes.shape[2]
    slot_count = hop_two.shape[2]
    all_rows = groups * block_rows
    node_ids = block_nodes.reshape(all_rows)
    own_part = jnp.take(features, node_ids, axis=1)
    neigh_ids = jnp.transpose(hop_two[:, 0], (1, 0, 2)).reshape(slot_count, all_rows)
    counts = hop_two_count.reshape(all_rows)
    gathered = jnp.take(features, neigh_ids, axis=1)
    usable = jnp.arange(slot_count, dtype=jnp.int32)[:, None] < counts[None, :]
    summed = jnp.sum(
        jnp.where(usable[None], gathered, jnp.zeros((), jnp.bfloat16)), axis=1, dtype=jnp.float32
    )
    mean_part = (summed / counts.astype(jnp.float32)[None, :]).astype(jnp.bfloat16)
    stacked = jnp.stack([own_part, mean_part])
    owned_rows = lax.all_to_all(
        stacked.reshape(2, feature_depth, groups, block_rows),
        "col",
        split_axis=2,
        concat_axis=1,
        tiled=True,
    ).reshape(2, feature_depth * groups, block_rows)
    pre_one = lax.dot_general(
        owned_rows,
        lax.all_gather(weight_one, "col", axis=1, tiled=True),
        (((0, 1), (0, 1)), ((), ())),
        preferred_element_type=jnp.float32,
    )
    hidden = (pre_one * jax.nn.sigmoid(pre_one)).astype(jnp.bfloat16)
    chosen = hop_one[0, 0]
    chosen_count = hop_one_count[0, 0]
    fan_first = chosen.shape[0]
    seed_number = chosen.shape[1]
    usable_one = jnp.arange(fan_first, dtype=jnp.int32)[:, None] < chosen_count[None, :]
    match = chosen[:, :, None] == jnp.arange(block_rows, dtype=jnp.int32)[None, None, :]
    adjacency = jnp.sum((match & usable_one[:, :, None]).astype(jnp.float32), axis=0)
    seed_count = chosen_count.astype(jnp.float32)[:, None]
    mean_two = (
        jnp.dot(adjacency.astype(jnp.bfloat16), hidden, preferred_element_type=jnp.float32)
        / seed_count
    ).astype(jnp.bfloat16)
    seed_rows = hidden[:seed_number]
    pre_two = jnp.dot(seed_rows, weight_two[0], preferred_element_type=jnp.float32) + jnp.dot(
        mean_two, weight_two[1], preferred_element_type=jnp.float32
    )
    hidden_two = (pre_two * jax.nn.sigmoid(pre_two)).astype(jnp.bfloat16)
    logits = jnp.dot(hidden_two, weight_three, preferred_element_type=jnp.float32)
    target = labels[0, 0].astype(jnp.float32)
    mean_loss = jnp.mean(jax.nn.softplus(logits) - target * logits)
    grad_logits = ((jax.nn.sigmoid(logits) - target) / seed_number).astype(jnp.bfloat16)
    grad_three = jnp.dot(hidden_two.T, grad_logits, preferred_element_type=jnp.float32)
    back_two = jnp.dot(grad_logits, weight_three.T, preferred_element_type=jnp.float32)
    grad_pre_two = (back_two * silu_slope(pre_two)).astype(jnp.bfloat16)
    grad_two = jnp.stack(
        [
            jnp.dot(seed_rows.T, grad_pre_two, preferred_element_type=jnp.float32),
            jnp.dot(mean_two.T, grad_pre_two, preferred_element_type=jnp.float32),
        ]
    )
    to_seeds = jnp.dot(grad_pre_two, weight_two[0].T, preferred_element_type=jnp.float32)
    to_means = (
        jnp.dot(grad_pre_two, weight_two[1].T, preferred_element_type=jnp.float32) / seed_count
    )
    grad_hidden = jnp.dot(adjacency.T, to_means, precision=lax.Precision.HIGHEST)
    grad_hidden = grad_hidden + jnp.concatenate(
        [to_seeds, jnp.zeros((block_rows - seed_number, width), jnp.float32)], axis=0
    )
    grad_pre_one = (grad_hidden * silu_slope(pre_one)).astype(jnp.bfloat16)
    grad_one = jnp.transpose(
        lax.psum_scatter(
            jnp.einsum("kfr,rh->fkh", owned_rows, grad_pre_one, preferred_element_type=jnp.float32),
            "col",
            scatter_dimension=0,
            tiled=True,
        ),
        (1, 0, 2),
    )
    grad_one = lax.psum(grad_one, "sub")
    grad_two, grad_three = lax.psum((grad_two, grad_three), ("col", "sub"))
    return (
        hidden.reshape(1, 1, block_rows, width),
        mean_loss.reshape(1, 1),
        grad_one,
        grad_two,
        grad_three,
    )


def solution(mesh):
    return jax.shard_map(
        per_device,
        mesh=mesh,
        in_specs=(
            P("col", "grp"),
            P("grp", "sub", None),
            P("grp", "sub", None, None),
            P("grp", "sub", None),
            P(("grp", "col"), "sub", None, None),
            P(("grp", "col"), "sub", None),
            P(("grp", "col"), "sub", None, None),
            P(None, "col", None),
            P(),
            P(),
        ),
        out_specs=(
            P(("grp", "col"), "sub", None, None),
            P(("grp", "col"), "sub"),
            P("grp", "col", None),
            P("grp", None, None),
            P("grp", None),
        ),
        check_vma=False,
    )
```

profile of v0, /device:TPU:0, one launch (start us, length us, event | category | flops | bytes accessed | tf_op | source)
XLA Modules:
  0.0 269.9 jit_solution(17443959811500677171)
XLA Ops:
  7.2 0.0 copy-start
  7.2 0.0 all-gather.2.cloned.1.call-start
  7.2 0.7 all-gather.2.cloned.1.call-update
  7.9 0.8 copy.39
  8.7 0.1 reshape.349
  8.8 0.1 reshape.350
  8.9 0.5 broadcast.220
  9.4 1.4 fusion.31
  10.8 0.1 lt.83
  10.9 0.0 copy-start.3
  10.9 0.0 copy-start.5
  10.9 0.0 copy-start.1
  10.9 0.0 copy-start.4
  10.9 22.5 %copy.32 = bf16[128,65536]{0,1:T(8,128)(2,1)} copy(bf16[128,65536]{1,0:T(8,128)(2,1)} %param.10) | data formatting | bytes 33554432 | tf_op args[0]
  33.4 0.0 copy-done.3
  33.4 0.7 reduce.14
  34.0 0.1 reshape.348
  34.1 12.3 %gather_fusion.1 = bf16[2560,128]{1,0:T(8,128)(2,1)S(1)} fusion(bf16[128,65536]{0,1:T(8,128)(2,1)} %copy.32, s32[3072]{0:T(1024)S(1)} %pad_clamp_fusion), kind=kCustom, calls=%fused_computation.1 | custom fusion | bytes 1320960 | tf_op jit(solution)/shard_map/jit(_take)/gather | solution.py:34
  46.4 8.7 %gather_fusion = bf16[256,128]{1,0:T(8,128)(2,1)S(1)} fusion(bf16[128,65536]{0,1:T(8,128)(2,1)} %copy.32, s32[1024]{0:T(1024)S(1)} %pad_clamp_fusion.1), kind=kCustom, calls=%fused_computation | custom fusion | bytes 132096 | tf_op jit(solution)/shard_map/jit(_take)/gather | solution.py:31
  55.1 1.0 convert_reduce_fusion
  56.2 0.1 broadcast_select_fusion
  56.3 0.1 divide_convert_fusion
  56.4 0.7 copy.35
  57.1 7.2 %all-to-all-start = ((bf16[2,128,8,32]{1,3,0,2:T(8,128)(2,1)}), bf16[2,128,8,32]{1,3,0,2:T(8,128)(2,1)S(1)}, u32[]{:S(2)}, u32[]{:S(2)}) async-start(bf16[2,128,8,32]{1,3,0,2:T(8,128)(2,1)} %copy.35), calls=%async_computation | async-start | bytes 262144 | tf_op jit(solution)/shard_map/all_to_all | solution.py:41
  64.3 0.0 reduce-scatter.2.cloned.1.call-start
  65.0 0.0 copy-done.5
  65.0 0.1 fusion.15
  65.2 6.5 %all-to-all-done = bf16[2,128,8,32]{1,3,0,2:T(8,128)(2,1)S(1)} async-done(((bf16[2,128,8,32]{1,3,0,2:T(8,128)(2,1)}), bf16[2,128,8,32]{1,3,0,2:T(8,128)(2,1)S(1)}, u32[]{:S(2)}, u32[]{:S(2)}) %all-to-all-start) | async-done | bytes 131104 | tf_op jit(solution)/shard_map/all_to_all | solution.py:41
  71.7 0.1 copy.36
  71.8 0.1 reshape.351
  71.8 0.0 all-gather.2.cloned.1.call-done
  71.9 1.5 multiply_convert_fusion.1
  73.4 0.0 copy-start.2
  73.4 0.1 fusion.21
  73.5 0.0 copy-done.1
  73.6 0.1 fusion.6
  73.7 0.1 fusion.2
  73.9 0.0 copy-done
  73.9 0.0 copy-done.4
  73.9 0.8 convert_convert_fusion
  74.7 0.1 fusion.19
  74.8 0.2 fusion
  75.0 0.2 fusion.4
  75.2 1.9 convolution_bitcast_fusion
  77.1 0.0 reduce-scatter.2.cloned.1.call-update
  77.1 0.0 all-reduce.5.cloned.1.call-start
  77.2 0.1 multiply_bitcast_fusion.1
  77.3 65.9 %reduce-scatter.2.cloned.1.call-done = f32[128,2,256]{0,2,1:T(8,128)} async-done(((f32[1024,2,256]{0,2,1:T(8,128)}), f32[128,2,256]{0,2,1:T(8,128)}) %reduce-scatter.2.cloned.1.call-update) | async-done | bytes 262160 | tf_op jit(solution)/shard_map/reduce_scatter | solution.py:95
  143.2 0.0 all-reduce.5.cloned.1.call-update
  143.2 0.0 all-reduce.7.cloned.1.call-start
  143.3 0.8 pad_maximum_fusion
  144.1 0.7 broadcast_multiply_fusion
  144.8 0.0 all-reduce.7.cloned.1.call-update
  145.5 17.3 %all-reduce.5.cloned.1.call-done = f32[2,128,256]{1,2,0:T(8,128)} async-done(((f32[2,128,256]{1,2,0:T(8,128)}), f32[2,128,256]{1,2,0:T(8,128)}) %all-reduce.5.cloned.1.call-update) | async-done | bytes 262160 | tf_op jit(solution)/shard_map/psum | solution.py:103
  162.8 1.8 copy.37
  164.6 94.2 %all-reduce.7.cloned.1.call-done = (f32[2,256,256]{2,1,0:T(8,128)}, f32[256,112]{0,1:T(8,128)}) async-done(((f32[2,256,256]{2,1,0:T(8,128)}, f32[256,112]{0,1:T(8,128)}), (f32[2,256,256]{2,1,0:T(8,128)}, f32[256,112]{0,1:T(8,128)})) %all-reduce.7.cloned.1.call-update) | async-done | bytes 638992 | tf_op jit(solution)/shard_map/psum | solution.py:104
  258.8 1.9 copy.44
  260.6 1.6 copy.45
  262.2 0.0 copy-done.2
  (18 shorter events, 0.2 us)
Async XLA Ops:
  7.2 66.7 %copy-start = (bf16[256,112]{0,1:T(8,128)(2,1)S(1)}, bf16[256,112]{0,1:T(8,128)(2,1)}, u32[]{:S(2)}) copy-start(bf16[256,112]{0,1:T(8,128)(2,1)} %param.19) | copy-start | bytes 172036
  7.2 64.7 %all-gather.2.cloned.1.call-start = ((), (), s32[]{:S(2)}) async-start(), calls=%async_computation.2 | async-start | bytes 1179648 | tf_op jit(solution)/shard_map/all_gather | solution.py:50
  10.9 22.5 %copy-start.3 = (s32[8,1,32]{2,1,0:T(1,128)S(1)}, s32[8,1,32]{2,1,0:T(1,128)}, u32[]{:S(2)}) copy-start(s32[8,1,32]{2,1,0:T(1,128)} %param.11) | copy-start | bytes 3076
  10.9 54.2 %copy-start.5 = (s32[1,1,25,1]{2,3,1,0:T(1,128)S(1)}, s32[1,1,25,1]{2,3,1,0:T(1,128)}, u32[]{:S(2)}) copy-start(s32[1,1,25,1]{2,3,1,0:T(1,128)} %param.14) | copy-start | bytes 304
  10.9 62.7 %copy-start.1 = (bf16[2,256,256]{2,1,0:T(8,128)(2,1)S(1)}, bf16[2,256,256]{2,1,0:T(8,128)(2,1)}, u32[]{:S(2)}) copy-start(bf16[2,256,256]{2,1,0:T(8,128)(2,1)} %param.18) | copy-start | bytes 786436
  10.9 63.0 %copy-start.4 = (s32[1,1,1,112]{3,2,1,0:T(1,128)S(1)}, s32[1,1,1,112]{3,2,1,0:T(1,128)}, u32[]{:S(2)}) copy-start(s32[1,1,1,112]{3,2,1,0:T(1,128)} %param.16) | copy-start | bytes 1348
  57.1 14.6 %all-to-all-start = ((bf16[2,128,8,32]{1,3,0,2:T(8,128)(2,1)}), bf16[2,128,8,32]{1,3,0,2:T(8,128)(2,1)S(1)}, u32[]{:S(2)}, u32[]{:S(2)}) async-start(bf16[2,128,8,32]{1,3,0,2:T(8,128)(2,1)} %copy.35), calls=%async_computation | async-start | bytes 262144 | tf_op jit(solution)/shard_map/all_to_all | solution.py:41
  64.3 78.9 %reduce-scatter.2.cloned.1.call-start = ((), (), s32[]{:S(2)}) async-start(), calls=%async_computation.3 | async-start | bytes 2359296 | tf_op jit(solution)/shard_map/reduce_scatter | solution.py:95
  73.4 188.8 %copy-start.2 = (bf16[32,256]{1,0:T(8,128)(2,1)}, bf16[32,256]{1,0:T(8,128)(2,1)S(1)}, u32[]{:S(2)}) copy-start(bf16[32,256]{1,0:T(8,128)(2,1)S(1)} %get-tuple-element.39) | copy-start | bytes 49156
  77.1 85.7 %all-reduce.5.cloned.1.call-start = ((), (), s32[]{:S(2)}) async-start(), calls=%async_computation.4 | async-start | bytes 524288 | tf_op jit(solution)/shard_map/psum | solution.py:103
  143.2 115.6 %all-reduce.7.cloned.1.call-start = ((), (), s32[]{:S(2)}) async-start(), calls=%async_computation.5 | async-start | bytes 1277952 | tf_op jit(solution)/shard_map/psum | solution.py:104
Sparse Core Ops, SparseCore 0:
  10.2 42.8 all-gather.1
  77.2 65.9 reduce-scatter.1
  145.5 17.2 all-reduce.4
  167.1 91.6 all-reduce.6
where the time goes:
time: 271 us; the launch traced here: 270 us
  waiting for transfers between devices  185 us (68%)
  local copies, waits for them, and re-layouts  51.1 us (19%)
  between operations  16.4 us (6%)
  starting transfers between devices  7.39 us (3%)
  other arithmetic  5.24 us (2%)
  matrix products  5.06 us (2%)
    psum x1, waiting for transfers between devices, per_device(): grad_two, grad_three = lax.psum((grad_two, grad_three), ('col', 'sub'))  94.2 us
    reduce_scatter x1, waiting for transfers between devices, per_device(): lax.psum_scatter(jnp.einsum('kfr,rh->fkh', owned_rows, grad_pre_one, pref...  65.9 us
    unnamed x18, local copies, waits for them, and re-layouts  29 us
    psum x1, waiting for transfers between devices, per_device(): grad_one = lax.psum(grad_one, 'sub')  17.3 us
    gather x1, local copies, waits for them, and re-layouts, per_device(): gathered = jnp.take(features, neigh_ids, axis=1)  12.3 us
    gather x1, local copies, waits for them, and re-layouts, per_device(): own_part = jnp.take(features, node_ids, axis=1)  8.69 us
    all_to_all x1, starting transfers between devices, per_device(): lax.all_to_all(stacked.reshape(2, feature_depth, groups, block_rows), 'co...  7.24 us
    all_to_all x1, waiting for transfers between devices, per_device(): lax.all_to_all(stacked.reshape(2, feature_depth, groups, block_rows), 'co...  6.49 us
  transfers between devices with their start and end apart: 5, of which 4 were waited for; matrix products, arithmetic and copies ran while one was open for 20% of the time, Pallas kernels for 0%

commit v1 on v0

v1 whole, which is shorter than its diff:
```python
import functools

import jax
import jax.numpy as jnp
from jax import lax
from jax.experimental import pallas as pl
from jax.experimental.pallas import tpu as pltpu
from jax.sharding import PartitionSpec as P

BF = jnp.bfloat16
F32 = jnp.float32
VMEM = pl.BlockSpec(memory_space=pltpu.VMEM)
SMEM = pl.BlockSpec(memory_space=pltpu.SMEM)
ANY = pl.BlockSpec(memory_space=pl.ANY)
NN = (((1,), (0,)), ((), ()))
NT = (((1,), (1,)), ((), ()))
TN = (((0,), (0,)), ((), ()))


def dot(a, b, dims=NN, **kw):
    return lax.dot_general(a, b, dims, preferred_element_type=F32, **kw)


def silu_slope(value, sig):
    return sig * (1.0 + value * (1.0 - sig))


def gather_kernel(
    chunks, slots, block, unroll, ids, counts, weights, meta, features, own_ref, mean_ref, pre_ref,
    stage, rows_f32, sums, sems,
):
    nodes = features.shape[1]
    span = nodes // chunks
    depth = features.shape[0]
    count_rows = own_ref.shape[0]
    per_row = ids.shape[0] // count_rows

    def fetch(k, slot):
        return pltpu.make_async_copy(
            features.at[:, pl.ds(pl.multiple_of(k * span, span), span)], stage.at[slot], sems.at[slot]
        )

    for k in range(slots):
        fetch(k, k).start()
    rows_f32[pl.ds(nodes, 8), :] = jnp.zeros((8, depth), F32)

    def chunk(k, carry):
        slot = lax.rem(k, slots)
        fetch(k, slot).wait()

        def turn(i, carry):
            for u in range(unroll):
                at = pl.multiple_of((i * unroll + u) * block, block)
                part = stage[slot, :, pl.ds(at, block)]
                if depth % 128 == 0:
                    flipped = part.T.astype(F32)
                else:
                    flipped = part.astype(F32).T
                rows_f32[pl.ds(pl.multiple_of(k * span + at, block), block), :] = flipped
            return carry

        lax.fori_loop(0, span // block // unroll, turn, 0)

        @pl.when(k + slots < chunks)
        def _():
            fetch(k + slots, slot).start()

        return carry

    lax.fori_loop(0, chunks, chunk, 0)

    def take(g, carry):
        for q in range(8):
            base = (g * 8 + q) * per_row
            sums[g, 0, q : q + 1, :] = rows_f32[pl.ds(ids[base], 1), :]
            total = rows_f32[pl.ds(ids[base + 1], 1), :]
            for j in range(2, per_row):
                total = total + rows_f32[pl.ds(ids[base + j], 1), :]
            sums[g, 1, q : q + 1, :] = total
        return carry

    lax.fori_loop(0, count_rows // 8, take, 0)
    own = sums[:, 0].reshape(count_rows, depth).astype(BF)
    mean = (sums[:, 1].reshape(count_rows, depth) / counts[...]).astype(BF)
    own_ref[...] = own
    mean_ref[...] = mean
    pre_ref[:count_rows, :] = (dot(own, weights[0]) + dot(mean, weights[1])).astype(BF)
    pre_ref[count_rows:, :] = meta[...]


def upper_kernel(
    block_rows, labels_at, mine, theirs, w_two, w_three, hidden_ref, loss_ref, pack_ref
):
    rows = hidden_ref.shape[0]
    batches = rows // block_rows
    label_count = w_three.shape[1]
    pre_one = mine[:rows, :].astype(F32) + theirs[:rows, :].astype(F32)
    meta = (mine[rows:, :].astype(F32) + theirs[rows:, :].astype(F32))[:batches]
    sig_one = jax.nn.sigmoid(pre_one)
    hidden = (pre_one * sig_one).astype(BF)
    hidden_ref[...] = hidden
    counts = meta[:, block_rows : block_rows + 1]
    target = meta[:, labels_at : labels_at + label_count]
    batch = lax.broadcasted_iota(jnp.int32, (batches, rows), 0)
    row = lax.broadcasted_iota(jnp.int32, (batches, rows), 1)
    tiled = jnp.concatenate([meta[:, :block_rows]] * batches, axis=1)
    adjacency = jnp.where(row // block_rows == batch, tiled, 0.0)
    first = jnp.where(row == batch * block_rows, 1.0, 0.0)
    seeds = dot(first.astype(BF), hidden).astype(BF)
    mean_two = (dot(adjacency.astype(BF), hidden) / counts).astype(BF)
    pre_two = dot(seeds, w_two[0]) + dot(mean_two, w_two[1])
    sig_two = jax.nn.sigmoid(pre_two)
    hidden_two = (pre_two * sig_two).astype(BF)
    logits = dot(hidden_two, w_three[...])
    soft = jnp.maximum(logits, 0.0) + jnp.log1p(jnp.exp(-jnp.abs(logits)))
    loss_ref[...] = jnp.mean(soft - target * logits, axis=1, keepdims=True)
    grad_logits = (jax.nn.sigmoid(logits) - target).astype(BF)
    back_two = dot(grad_logits, w_three[...], NT)
    grad_two = (back_two * silu_slope(pre_two, sig_two)).astype(BF)
    to_seeds = dot(grad_two, w_two[0], NT)
    to_means = dot(grad_two, w_two[1], NT) / counts
    grad_hidden = lax.dot_general(
        jnp.concatenate([adjacency, first], axis=0),
        jnp.concatenate([to_means, to_seeds], axis=0),
        TN,
        precision=lax.Precision.HIGHEST,
        preferred_element_type=F32,
    )
    pack_ref[:rows, :] = (grad_hidden * silu_slope(pre_one, sig_one)).astype(BF)
    width = hidden.shape[1]
    blank = jnp.zeros((batches, width - label_count), F32)
    tail = jnp.concatenate(
        [
            seeds.astype(F32),
            mean_two.astype(F32),
            grad_two.astype(F32),
            hidden_two.astype(F32),
            jnp.concatenate([grad_logits.astype(F32), blank], axis=1),
            jnp.zeros((batches, width), F32),
        ],
        axis=0,
    )
    pack_ref[rows:, :] = tail.astype(BF)


def final_kernel(
    batches, label_count, own_a, mean_a, pack_a, own_b, mean_b, pack_b, one_ref, two_ref, three_ref
):
    rows = own_a.shape[0]

    def part(pack, k):
        at = rows + k * batches
        if batches % 16 == 0:
            return pack[at : at + batches, :]
        return pack[rows:, :].astype(F32)[k * batches : (k + 1) * batches].astype(BF)

    grad_a, grad_b = pack_a[:rows, :], pack_b[:rows, :]
    one_ref[0] = dot(own_a[...], grad_a, TN) + dot(own_b[...], grad_b, TN)
    one_ref[1] = dot(mean_a[...], grad_a, TN) + dot(mean_b[...], grad_b, TN)
    for k in range(2):
        two_ref[k] = dot(part(pack_a, k), part(pack_a, 2), TN) + dot(part(pack_b, k), part(pack_b, 2), TN)
    three = dot(part(pack_a, 3), part(pack_a, 4), TN) + dot(part(pack_b, 3), part(pack_b, 4), TN)
    three_ref[...] = three[:, :label_count]


def per_device(
    features,
    block_nodes,
    hop_two,
    hop_two_count,
    hop_one,
    hop_one_count,
    labels,
    weight_one,
    weight_two,
    weight_three,
):
    groups = lax.axis_size("col")
    me = lax.axis_index("col")
    depth, nodes = features.shape
    width = weight_one.shape[2]
    block_rows = block_nodes.shape[2]
    slot_count = hop_two.shape[2]
    label_count = weight_three.shape[1]
    rows = groups * block_rows

    counts = hop_two_count.reshape(groups, block_rows)
    usable = jnp.arange(slot_count, dtype=jnp.int32)[None, :, None] < counts[:, None, :]
    neighbours = jnp.where(usable, hop_two[:, 0], nodes)
    ids = jnp.concatenate([block_nodes, neighbours], axis=1)
    ids = jnp.transpose(ids, (0, 2, 1)).reshape(rows * (slot_count + 1))

    fan_first = hop_one.shape[2]
    usable_one = jnp.arange(fan_first, dtype=jnp.int32) < hop_one_count[0, 0, 0]
    match = hop_one[0, 0] == jnp.arange(block_rows, dtype=jnp.int32)[None, :]
    adjacency = jnp.sum((match & usable_one[:, None]).astype(F32), axis=0)
    labels_at = width // 2
    mine = jnp.concatenate(
        [
            adjacency,
            hop_one_count[0, 0].astype(F32),
            jnp.zeros((labels_at - block_rows - 1,), F32),
            labels[0, 0, 0].astype(F32),
            jnp.zeros((width - labels_at - label_count,), F32),
        ]
    )
    meta_rows = -(-groups // 16) * 16
    slot = jnp.arange(meta_rows, dtype=jnp.int32)[:, None] == me
    meta = jnp.where(slot, mine[None, :], 0.0).astype(BF)

    chunks = 16
    own, mean, pre = pl.pallas_call(
        functools.partial(gather_kernel, chunks, 8, 256, 16),
        out_shape=(
            jax.ShapeDtypeStruct((rows, depth), BF),
            jax.ShapeDtypeStruct((rows, depth), BF),
            jax.ShapeDtypeStruct((rows + meta_rows, width), BF),
        ),
        in_specs=[SMEM, VMEM, VMEM, VMEM, ANY],
        out_specs=(VMEM, VMEM, VMEM),
        scratch_shapes=[
            pltpu.VMEM((8, depth, nodes // chunks), BF),
            pltpu.VMEM((nodes + 8, depth), F32),
            pltpu.VMEM((rows // 8, 2, 8, depth), F32),
            pltpu.SemaphoreType.DMA((8,)),
        ],
        compiler_params=pltpu.CompilerParams(vmem_limit_bytes=56 * 2**20),
    )(ids, counts.reshape(rows, 1).astype(F32), weight_one, meta, features)

    swap = [(0, 1), (1, 0)]
    own_b = lax.ppermute(own, "sub", swap)
    mean_b = lax.ppermute(mean, "sub", swap)
    bit = 1
    while bit < groups:
        other = lax.ppermute(pre, "col", [(i, i ^ bit) for i in range(groups)])
        bit *= 2
        if bit < groups:
            pre = (pre.astype(F32) + other.astype(F32)).astype(BF)

    hidden, loss, pack = pl.pallas_call(
        functools.partial(upper_kernel, block_rows, labels_at),
        out_shape=(
            jax.ShapeDtypeStruct((rows, width), BF),
            jax.ShapeDtypeStruct((groups, 1), F32),
            jax.ShapeDtypeStruct((rows + 6 * groups, width), BF),
        ),
        in_specs=[VMEM] * 4,
        out_specs=(VMEM, VMEM, VMEM),
        compiler_params=pltpu.CompilerParams(vmem_limit_bytes=56 * 2**20),
    )(pre, other, weight_two, weight_three)

    pack_b = lax.ppermute(pack, "sub", swap)
    grad_one, grad_two, grad_three = pl.pallas_call(
        functools.partial(final_kernel, groups, label_count),
        out_shape=(
            jax.ShapeDtypeStruct((2, depth, width), F32),
            jax.ShapeDtypeStruct((2, width, width), F32),
            jax.ShapeDtypeStruct((width, label_count), F32),
        ),
        in_specs=[VMEM] * 6,
        out_specs=(VMEM, VMEM, VMEM),
        compiler_params=pltpu.CompilerParams(vmem_limit_bytes=56 * 2**20),
    )(own, mean, pack, own_b, mean_b, pack_b)
    return (
        lax.dynamic_slice_in_dim(hidden, me * block_rows, block_rows, 0).reshape(1, 1, block_rows, width),
        lax.dynamic_slice_in_dim(loss, me, 1, 0),
        grad_one,
        grad_two,
        grad_three,
    )


def solution(mesh):
    return jax.shard_map(
        per_device,
        mesh=mesh,
        in_specs=(
            P("col", "grp"),
            P("grp", "sub", None),
            P("grp", "sub", None, None),
            P("grp", "sub", None),
            P(("grp", "col"), "sub", None, None),
            P(("grp", "col"), "sub", None),
            P(("grp", "col"), "sub", None, None),
            P(None, "col", None),
            P(),
            P(),
        ),
        out_specs=(
            P(("grp", "col"), "sub", None, None),
            P(("grp", "col"), "sub"),
            P("grp", "col", None),
            P("grp", None, None),
            P("grp", None),
        ),
        check_vma=False,
    )
```

time: 271 us -> 51.7 us (0.19)
  waiting for transfers between devices: 185 us -> 11.2 us
  local copies, waits for them, and re-layouts: 51.1 us -> 8.66 us
  Pallas kernels: 0 us -> 16.4 us
  between operations: 16.4 us -> 1.39 us
  matrix products: 5.06 us -> 0 us
    psum x2 -> x0, waiting for transfers between devices: 112 us -> none  [the longest x1 94.2 us: per_device(): grad_two, grad_three = lax.psum((grad_two, grad_three), ('col', 'sub'))]
    reduce_scatter x1 -> x0, waiting for transfers between devices: 65.9 us -> none  [per_device(): lax.psum_scatter(jnp.einsum('kfr,rh->fkh', owned_rows, grad_pre_one, pref...]
    unnamed x18 -> x14, local copies, waits for them, and re-layouts: 29 us -> 4.3 us
    gather x2 -> x0, local copies, waits for them, and re-layouts: 21 us -> none  [the longest x1 12.3 us: per_device(): gathered = jnp.take(features, neigh_ids, axis=1)]
    pallas_call x0 -> x3, Pallas kernels: none -> 16.4 us  [the longest x1 11 us: per_device(): pl.pallas_call(functools.partial(gather_kernel, chunks, 8, 256, 16), out_...]
    ppermute x0 -> x6, waiting for transfers between devices: none -> 11.2 us  [the longest x3 11.1 us: per_device(): other = lax.ppermute(pre, 'col', [(i, i ^ bit) for i in range(groups)])]
    ppermute x0 -> x6, starting transfers between devices: none -> 8.31 us  [the longest x3 7.8 us: per_device(): other = lax.ppermute(pre, 'col', [(i, i ^ bit) for i in range(groups)])]
    all_to_all x1 -> x0, starting transfers between devices: 7.24 us -> none  [per_device(): lax.all_to_all(stacked.reshape(2, feature_depth, groups, block_rows), 'co...]
  transfers between devices with their start and end apart: 5 -> 6, of which waited for: 4 -> 3; matrix products, arithmetic and copies ran while one was open for 20% -> 6% of each run, Pallas kernels for 0% -> 0%
where the time goes in v1:
time: 51.7 us; the launch traced here: 51.1 us
  Pallas kernels  16.4 us (32%)
  waiting for transfers between devices  11.2 us (22%)
  local copies, waits for them, and re-layouts  8.66 us (17%)
  starting transfers between devices  8.31 us (16%)
  other arithmetic  5.26 us (10%)
  between operations  1.39 us (3%)
    ppermute x3, waiting for transfers between devices, per_device(): other = lax.ppermute(pre, 'col', [(i, i ^ bit) for i in range(groups)])  11.1 us
    pallas_call x1, Pallas kernels, per_device(): pl.pallas_call(functools.partial(gather_kernel, chunks, 8, 256, 16), out_...  11 us
    ppermute x3, starting transfers between devices, per_device(): other = lax.ppermute(pre, 'col', [(i, i ^ bit) for i in range(groups)])  7.8 us
    unnamed x14, local copies, waits for them, and re-layouts  4.3 us
    pallas_call x1, Pallas kernels, per_device(): pl.pallas_call(functools.partial(upper_kernel, block_rows, labels_at), ou...  2.94 us
    pallas_call x1, Pallas kernels, per_device(): pl.pallas_call(functools.partial(final_kernel, groups, label_count), out_...  2.4 us
    reshape x1, local copies, waits for them, and re-layouts, per_device(): lax.dynamic_slice_in_dim(hidden, me * block_rows, block_rows, 0)  1.32 us
    dynamic_slice x1, local copies, waits for them, and re-layouts, per_device(): lax.dynamic_slice_in_dim(loss, me, 1, 0)  1.2 us
  transfers between devices with their start and end apart: 6, of which 3 were waited for; matrix products, arithmetic and copies ran while one was open for 6% of the time, Pallas kernels for 0%

profile of v1, /device:TPU:0, one launch (start us, length us, event | category | flops | bytes accessed | tf_op | source)
XLA Modules:
  0.0 51.1 jit_solution(5970052518847056728)
XLA Ops:
  0.6 0.0 copy-start.5
  1.3 0.7 %convert_bitcast_fusion = bf16[112]{0:T(256)(128)(2,1)S(1)} fusion(s32[1,1,1,112]{3,2,1,0:T(1,128)} %param.16), kind=kLoop, calls=%fused_computation.12 | loop fusion | flops 112 | bytes 672 | tf_op jit(solution)/shard_map/convert_element_type | solution.py:203
  2.0 0.7 %convert_reduce_fusion.1 = f32[8,32]{1,0:T(8,128)S(1)} fusion(s32[8,1,32]{2,1,0:T(1,128)} %param.13), kind=kLoop, calls=%fused_computation.10 | loop fusion | flops 256 | bytes 2048 | tf_op jit(solution)/shard_map/convert_element_type | solution.py:228
  2.7 0.8 %bitcast_select_fusion = s32[8,10,32]{2,0,1:T(8,128)S(1)} fusion(s32[8,1,10,32]{3,1,2,0:T(1,128)} %param.12, s32[8,32]{1,0:T(8,128)} %bitcast.14), kind=kLoop, calls=%fused_computation.3 | loop fusion | flops 5120 | bytes 21504 | tf_op jit(solution)/shard_map/jit(_where)/select_n | solution.py:189
  3.5 0.7 %add_bitcast_fusion = s32[8,32,11]{1,0,2:T(8,128)S(1)} fusion(s32[8,10,32]{2,0,1:T(8,128)S(1)} %bitcast_select_fusion, s32[8,1,32]{2,0,1:T(8,128)} %bitcast.15), kind=kLoop, calls=%fused_computation.2 | loop fusion | flops 2816 | bytes 22528 | tf_op jit(solution)/shard_map/transpose | solution.py:191
  4.2 0.1 copy.25
  4.3 0.8 %reshape.42.ids = s32[2816]{0:T(1024)} reshape(s32[8,32,11]{2,1,0:T(8,128)S(1)} %copy.25) | data formatting | bytes 22528 | tf_op jit(solution)/shard_map/reshape | solution.py:191
  5.1 0.8 %convert_element_type.55.counts = f32[256,1]{1,0:T(8,128)} reshape(f32[8,32]{1,0:T(8,128)S(1)} %convert_reduce_fusion.1) | data formatting | bytes 2048 | tf_op jit(solution)/shard_map/convert_element_type | solution.py:228
  5.9 0.7 %convert_reduce_fusion = bf16[32]{0:T(256)(128)(2,1)S(1)} fusion(s32[25]{0:T(128)} %bitcast.16, pred[25]{0:T(512)(128)(4,1)S(1)} %iota_compare_fusion.2), kind=kLoop, calls=%fused_computation.7 | loop fusion | flops 3168 | bytes 189 | tf_op jit(solution)/shard_map/reduce_sum | solution.py:196
  6.7 0.1 concatenate.7
  6.8 0.7 %select_convert_fusion.meta = bf16[16,256]{1,0:T(8,128)(2,1)} fusion(bf16[256]{0:T(256)(128)(2,1)S(1)} %concatenate.7, pred[16]{0:T(512)(128)(4,1)S(1)} %iota_compare_fusion.3), kind=kLoop, calls=%fused_computation.6 | loop fusion | flops 4096 | bytes 8720 | tf_op jit(solution)/shard_map/convert_element_type | solution.py:209
  7.4 11.0 %shard_map.137 = (bf16[256,128]{1,0:T(8,128)(2,1)}, bf16[256,128]{1,0:T(8,128)(2,1)}, bf16[272,256]{1,0:T(8,128)(2,1)}) custom-call(s32[2816]{0:T(1024)} %reshape.42.ids, f32[256,1]{1,0:T(8,128)} %convert_element_type.55.counts, bf16[2,128,256]{2,1,0:T(8,128)(2,1)} %weights.1, bf16[16,256]{1,0:T(8,128)(2,1)} %select_convert_fusion.meta, ...), custom_call_target="tpu_custom_call" | custom-call | tf_op jit(solution)/shard_map/pallas_call | solution.py:212
  18.5 3.0 %collective-permute-start = (bf16[272,256]{1,0:T(8,128)(2,1)}, bf16[272,256]{1,0:T(8,128)(2,1)S(1)}, u32[]{:S(2)}, u32[]{:S(2)}) collective-permute-start(bf16[272,256]{1,0:T(8,128)(2,1)} %get-tuple-element.14), channel_id=1, source_target_pairs={{0,2},{2,0},{4,6},{6,4},{8,10},{10,8},{12,14},{14,12},{1,3},{3,1},... | collective-permute-start | bytes 417800 | tf_op jit(solution)/shard_map/ppermute | solution.py:235
  21.5 3.9 %collective-permute-done = bf16[272,256]{1,0:T(8,128)(2,1)S(1)} collective-permute-done((bf16[272,256]{1,0:T(8,128)(2,1)}, bf16[272,256]{1,0:T(8,128)(2,1)S(1)}, u32[]{:S(2)}, u32[]{:S(2)}) %collective-permute-start) | collective-permute-done | bytes 139296 | tf_op jit(solution)/shard_map/ppermute | solution.py:235
  25.4 0.9 %add_convert_fusion.1 = bf16[272,256]{1,0:T(8,128)(2,1)S(1)} fusion(bf16[272,256]{1,0:T(8,128)(2,1)S(1)} %collective-permute-done, bf16[272,256]{1,0:T(8,128)(2,1)} %get-tuple-element.14), kind=kLoop, calls=%fused_computation.1 | loop fusion | flops 278528 | bytes 417792 | tf_op jit(solution)/shard_map/convert_element_type | solution.py:238
  26.3 1.9 %collective-permute-start.1 = (bf16[272,256]{1,0:T(8,128)(2,1)S(1)}, bf16[272,256]{1,0:T(8,128)(2,1)S(1)}, u32[]{:S(2)}, u32[]{:S(2)}) collective-permute-start(bf16[272,256]{1,0:T(8,128)(2,1)S(1)} %add_convert_fusion.1), channel_id=1, source_target_pairs={{0,4},{2,6},{4,0},{6,2},{8,12},{10,14},{12,8},{14,10},{1,5},{3,7},... | collective-permute-start | bytes 417800 | tf_op jit(solution)/shard_map/ppermute | solution.py:235
  28.2 3.2 %collective-permute-done.1 = bf16[272,256]{1,0:T(8,128)(2,1)S(1)} collective-permute-done((bf16[272,256]{1,0:T(8,128)(2,1)S(1)}, bf16[272,256]{1,0:T(8,128)(2,1)S(1)}, u32[]{:S(2)}, u32[]{:S(2)}) %collective-permute-start.1) | collective-permute-done | bytes 139296 | tf_op jit(solution)/shard_map/ppermute | solution.py:235
  31.5 0.0 copy-start
  31.5 2.9 %collective-permute-start.2 = (bf16[272,256]{1,0:T(8,128)(2,1)S(1)}, bf16[272,256]{1,0:T(8,128)(2,1)S(1)}, u32[]{:S(2)}, u32[]{:S(2)}) collective-permute-start(bf16[272,256]{1,0:T(8,128)(2,1)S(1)} %add_convert_fusion.mine), channel_id=1, source_target_pairs={{0,8},{2,10},{4,12},{6,14},{8,0},{10,2},{12,4},{14,6},{1,9},{3,11}... | collective-permute-start | bytes 417800 | tf_op jit(solution)/shard_map/ppermute | solution.py:235
  34.4 0.0 copy-done.5
  34.4 0.7 %copy.27.w_three = bf16[256,112]{1,0:T(8,128)(2,1)} copy(bf16[256,112]{0,1:T(8,128)(2,1)S(1)} %copy-done.5) | data formatting | bytes 114688 | tf_op args[9]
  35.1 4.0 %collective-permute-done.2.theirs = bf16[272,256]{1,0:T(8,128)(2,1)S(1)} collective-permute-done((bf16[272,256]{1,0:T(8,128)(2,1)S(1)}, bf16[272,256]{1,0:T(8,128)(2,1)S(1)}, u32[]{:S(2)}, u32[]{:S(2)}) %collective-permute-start.2) | collective-permute-done | bytes 139296 | tf_op jit(solution)/shard_map/ppermute | solution.py:235
  39.1 0.0 copy-done
  39.1 0.0 copy-start.2
  39.1 0.7 %copy-done.2 = bf16[272,256]{1,0:T(8,128)(2,1)} copy-done((bf16[272,256]{1,0:T(8,128)(2,1)}, bf16[272,256]{1,0:T(8,128)(2,1)S(1)}, u32[]{:S(2)}) %copy-start.2) | copy-done | bytes 139288
  39.8 2.9 %shard_map.138 = (bf16[256,256]{1,0:T(8,128)(2,1)}, f32[8,1]{1,0:T(8,128)}, bf16[304,256]{1,0:T(8,128)(2,1)}) custom-call(bf16[272,256]{1,0:T(8,128)(2,1)} %copy-done, bf16[272,256]{1,0:T(8,128)(2,1)} %copy-done.2, bf16[2,256,256]{2,1,0:T(8,128)(2,1)} %w_two.1, bf16[256,112]{1,0:T(8,128)(2,1)} %copy.27.w_three), custom_call_target="tpu_custom_call" | custom-call | tf_op jit(solution)/shard_map/pallas_call | solution.py:240
  42.7 0.0 collective-permute-start.5
  42.7 0.5 collective-permute-start.3
  43.3 0.0 collective-permute-start.4
  43.3 1.2 %constant_dynamic-slice_fusion = f32[1,1]{1,0:T(1,128)} fusion(f32[8,1]{1,0:T(8,128)} %get-tuple-element.16, s32[]{:T(128)S(6)} %select_n.17), kind=kLoop, calls=%fused_computation.11 | loop fusion | bytes 12 | tf_op jit(solution)/shard_map/dynamic_slice | solution.py:266
  44.5 1.3 %dynamic-slice_bitcast_fusion = bf16[1,1,32,256]{3,2,1,0:T(8,128)(2,1)} fusion(bf16[256,256]{1,0:T(8,128)(2,1)} %get-tuple-element.15, s32[]{:T(128)S(6)} %select_n.16), kind=kLoop, calls=%fused_computation.5 | loop fusion | bytes 32772 | tf_op jit(solution)/shard_map/reshape | solution.py:265
  45.8 0.0 collective-permute-done.3.own_b
  45.8 0.0 copy-start.3
  45.8 0.0 collective-permute-done.4.mean_b
  45.8 0.0 copy-start.4
  45.8 0.0 collective-permute-done.5.pack_b
  45.8 0.6 %copy-done.3 = bf16[256,128]{1,0:T(8,128)(2,1)} copy-done((bf16[256,128]{1,0:T(8,128)(2,1)}, bf16[256,128]{1,0:T(8,128)(2,1)S(1)}, u32[]{:S(2)}) %copy-start.3) | copy-done | bytes 65560
  46.4 0.0 copy-done.4
  46.4 0.0 copy-start.1
  46.4 0.7 %copy-done.1 = bf16[304,256]{1,0:T(8,128)(2,1)} copy-done((bf16[304,256]{1,0:T(8,128)(2,1)}, bf16[304,256]{1,0:T(8,128)(2,1)S(1)}, u32[]{:S(2)}) %copy-start.1) | copy-done | bytes 155672
  47.1 2.4 %shard_map.139 = (f32[2,128,256]{2,1,0:T(8,128)}, f32[2,256,256]{2,1,0:T(8,128)}, f32[256,112]{1,0:T(8,128)}) custom-call(bf16[256,128]{1,0:T(8,128)(2,1)} %get-tuple-element.17.own_a, bf16[256,128]{1,0:T(8,128)(2,1)} %get-tuple-element.18.mean_a, bf16[304,256]{1,0:T(8,128)(2,1)} %get-tuple-element.19.pack_a, bf16[256,128]{1,0:T(8,128)(2,1)} %copy-done.3, ...), custom_call_target="tpu_custom_call" | custom-call | tf_op jit(solution)/shard_map/pallas_call | solution.py:253
  49.5 1.6 %copy.28 = f32[256,112]{0,1:T(8,128)} copy(f32[256,112]{1,0:T(8,128)} %get-tuple-element.37) | data formatting | bytes 229376
  (5 shorter events, 0.1 us)
Async XLA Ops:
  0.6 33.8 %copy-start.5 = (bf16[256,112]{0,1:T(8,128)(2,1)S(1)}, bf16[256,112]{0,1:T(8,128)(2,1)}, u32[]{:S(2)}) copy-start(bf16[256,112]{0,1:T(8,128)(2,1)} %param.19) | copy-start | bytes 172036
  18.5 6.9 %collective-permute-start = (bf16[272,256]{1,0:T(8,128)(2,1)}, bf16[272,256]{1,0:T(8,128)(2,1)S(1)}, u32[]{:S(2)}, u32[]{:S(2)}) collective-permute-start(bf16[272,256]{1,0:T(8,128)(2,1)} %get-tuple-element.14), channel_id=1, source_target_pairs={{0,2},{2,0},{4,6},{6,4},{8,10},{10,8},{12,14},{14,12},{1,3},{3,1},... | collective-permute-start | bytes 417800 | tf_op jit(solution)/shard_map/ppermute | solution.py:235
  26.3 5.1 %collective-permute-start.1 = (bf16[272,256]{1,0:T(8,128)(2,1)S(1)}, bf16[272,256]{1,0:T(8,128)(2,1)S(1)}, u32[]{:S(2)}, u32[]{:S(2)}) collective-permute-start(bf16[272,256]{1,0:T(8,128)(2,1)S(1)} %add_convert_fusion.1), channel_id=1, source_target_pairs={{0,4},{2,6},{4,0},{6,2},{8,12},{10,14},{12,8},{14,10},{1,5},{3,7},... | collective-permute-start | bytes 417800 | tf_op jit(solution)/shard_map/ppermute | solution.py:235
  31.5 7.7 %copy-start = (bf16[272,256]{1,0:T(8,128)(2,1)}, bf16[272,256]{1,0:T(8,128)(2,1)S(1)}, u32[]{:S(2)}) copy-start(bf16[272,256]{1,0:T(8,128)(2,1)S(1)} %add_convert_fusion.mine) | copy-start | bytes 417796
  31.5 7.7 %collective-permute-start.2 = (bf16[272,256]{1,0:T(8,128)(2,1)S(1)}, bf16[272,256]{1,0:T(8,128)(2,1)S(1)}, u32[]{:S(2)}, u32[]{:S(2)}) collective-permute-start(bf16[272,256]{1,0:T(8,128)(2,1)S(1)} %add_convert_fusion.mine), channel_id=1, source_target_pairs={{0,8},{2,10},{4,12},{6,14},{8,0},{10,2},{12,4},{14,6},{1,9},{3,11}... | collective-permute-start | bytes 417800 | tf_op jit(solution)/shard_map/ppermute | solution.py:235
  39.1 0.7 %copy-start.2 = (bf16[272,256]{1,0:T(8,128)(2,1)}, bf16[272,256]{1,0:T(8,128)(2,1)S(1)}, u32[]{:S(2)}) copy-start(bf16[272,256]{1,0:T(8,128)(2,1)S(1)} %collective-permute-done.2.theirs) | copy-start | bytes 417796
  42.7 3.1 %collective-permute-start.5 = (bf16[304,256]{1,0:T(8,128)(2,1)}, bf16[304,256]{1,0:T(8,128)(2,1)S(1)}, u32[]{:S(2)}, u32[]{:S(2)}) collective-permute-start(bf16[304,256]{1,0:T(8,128)(2,1)} %get-tuple-element.19.pack_a), channel_id=1, source_target_pairs={{0,1},{1,0},{2,3},{3,2},{4,5},{5,4},{6,7},{7,6},{8,9},{9,8},{10,11... | collective-permute-start | bytes 466952 | tf_op jit(solution)/shard_map/ppermute | solution.py:252
  42.7 3.0 %collective-permute-start.3 = (bf16[256,128]{1,0:T(8,128)(2,1)}, bf16[256,128]{1,0:T(8,128)(2,1)S(1)}, u32[]{:S(2)}, u32[]{:S(2)}) collective-permute-start(bf16[256,128]{1,0:T(8,128)(2,1)} %get-tuple-element.17.own_a), channel_id=1, source_target_pairs={{0,1},{1,0},{2,3},{3,2},{4,5},{5,4},{6,7},{7,6},{8,9},{9,8},{10,11... | collective-permute-start | bytes 196616 | tf_op jit(solution)/shard_map/ppermute | solution.py:231
  43.3 2.5 %collective-permute-start.4 = (bf16[256,128]{1,0:T(8,128)(2,1)}, bf16[256,128]{1,0:T(8,128)(2,1)S(1)}, u32[]{:S(2)}, u32[]{:S(2)}) collective-permute-start(bf16[256,128]{1,0:T(8,128)(2,1)} %get-tuple-element.18.mean_a), channel_id=1, source_target_pairs={{0,1},{1,0},{2,3},{3,2},{4,5},{5,4},{6,7},{7,6},{8,9},{9,8},{10,11... | collective-permute-start | bytes 196616 | tf_op jit(solution)/shard_map/ppermute | solution.py:232
  45.8 0.6 %copy-start.3 = (bf16[256,128]{1,0:T(8,128)(2,1)}, bf16[256,128]{1,0:T(8,128)(2,1)S(1)}, u32[]{:S(2)}) copy-start(bf16[256,128]{1,0:T(8,128)(2,1)S(1)} %collective-permute-done.3.own_b) | copy-start | bytes 196612
  45.8 0.6 %copy-start.4 = (bf16[256,128]{1,0:T(8,128)(2,1)}, bf16[256,128]{1,0:T(8,128)(2,1)S(1)}, u32[]{:S(2)}) copy-start(bf16[256,128]{1,0:T(8,128)(2,1)S(1)} %collective-permute-done.4.mean_b) | copy-start | bytes 196612
  46.4 0.7 %copy-start.1 = (bf16[304,256]{1,0:T(8,128)(2,1)}, bf16[304,256]{1,0:T(8,128)(2,1)S(1)}, u32[]{:S(2)}) copy-start(bf16[304,256]{1,0:T(8,128)(2,1)S(1)} %collective-permute-done.5.pack_b) | copy-start | bytes 466948

commit v2 on v1

v2 whole, which is shorter than its diff:
```python
import functools

import jax
import jax.numpy as jnp
from jax import lax
from jax.experimental import pallas as pl
from jax.experimental.pallas import tpu as pltpu
from jax.sharding import PartitionSpec as P

BF = jnp.bfloat16
F32 = jnp.float32
VMEM = pl.BlockSpec(memory_space=pltpu.VMEM)
HBM = pl.BlockSpec(memory_space=pltpu.HBM)
SMEM = pl.BlockSpec(memory_space=pltpu.SMEM)
NN = (((1,), (0,)), ((), ()))
NT = (((1,), (1,)), ((), ()))
TN = (((0,), (0,)), ((), ()))


def dot(a, b, dims=NN, **kw):
    return lax.dot_general(a, b, dims, preferred_element_type=F32, **kw)


def add_up(terms):
    terms = [term.astype(F32) for term in terms]
    while len(terms) > 1:
        terms = [a + b for a, b in zip(terms[::2], terms[1::2])]
    return terms[0]


def phases(groups):
    bits = groups.bit_length() - 1
    plan = []
    if bits % 2:
        bits -= 1
        plan.append([(1 << bits) | (1 << bits >> 1)])
    while bits:
        bits -= 2
        plan.append([1 << bits, 2 << bits, 3 << bits])
    return plan


def silu_slope(value, sig):
    return sig * (1.0 + value * (1.0 - sig))


def gather_kernel(
    chunks, block, unroll, labels_at, own_ids, hop_ids, hop_counts, seed_hops, labels, weights, features,
    seed_count, parts_ref, pre_ref, stage, rows_f32, sums, own_s, hop_v, hop_s, count_v, seed_s, labels_v, weights_v,
    sems, small,
):
    depth, nodes = features.shape
    span = nodes // chunks
    slots = stage.shape[0]
    groups, _, block_rows = own_ids.shape
    fan = hop_ids.shape[1]
    rows = groups * block_rows
    width = weights.shape[2]

    def fetch(k, slot):
        at = pl.multiple_of(k * span, span)
        return pltpu.make_async_copy(features.at[:, pl.ds(at, span)], stage.at[slot], sems.at[slot])

    inputs = [
        pltpu.make_async_copy(source, target, small.at[k])
        for k, (source, target) in enumerate(
            (
                (hop_ids, hop_v),
                (hop_counts, count_v),
                (own_ids, own_s),
                (seed_hops, seed_s),
                (labels, labels_v),
                (weights, weights_v),
            )
        )
    ]
    inputs[0].start()
    inputs[1].start()
    for k in range(slots):
        fetch(k, k).start()
    for copy in inputs[2:]:
        copy.start()
    rows_f32[pl.ds(nodes, 8), :] = jnp.zeros((8, depth), F32)
    inputs[0].wait()
    inputs[1].wait()
    counts = count_v[...]
    slot_of = lax.broadcasted_iota(jnp.int32, hop_v.shape, 1)
    hop_v[...] = jnp.where(slot_of < counts[:, :, None, :], hop_v[...], nodes)
    to_scalars = pltpu.make_async_copy(hop_v, hop_s, small.at[len(inputs)])
    to_scalars.start()

    def chunk(k, carry):
        slot = lax.rem(k, slots)
        fetch(k, slot).wait()

        def turn(i, carry):
            for u in range(unroll):
                at = pl.multiple_of((i * unroll + u) * block, block)
                part = stage[slot, :, pl.ds(at, block)]
                if depth % 128 == 0:
                    flipped = part.T.astype(F32)
                else:
                    flipped = part.astype(F32).T
                rows_f32[pl.ds(pl.multiple_of(k * span + at, block), block), :] = flipped
            return carry

        lax.fori_loop(0, span // block // unroll, turn, 0)

        @pl.when(k + slots < chunks)
        def _():
            fetch(k + slots, slot).start()

        return carry

    lax.fori_loop(0, chunks, chunk, 0)
    for copy in inputs[2:]:
        copy.wait()
    to_scalars.wait()

    def take(b, carry):
        for r in range(block_rows):
            g, q = r // 8, r % 8
            sums[b, g, 0, q : q + 1, :] = rows_f32[pl.ds(own_s[b, 0, r], 1), :]
            total = rows_f32[pl.ds(hop_s[b, 0, 0, r], 1), :]
            for j in range(1, fan):
                total = total + rows_f32[pl.ds(hop_s[b, j, 0, r], 1), :]
            sums[b, g, 1, q : q + 1, :] = total
        return carry

    lax.fori_loop(0, groups, take, 0)
    member = lax.broadcasted_iota(jnp.int32, (rows, groups), 0) // block_rows
    member = jnp.where(member == lax.broadcasted_iota(jnp.int32, (rows, groups), 1), 1.0, 0.0).astype(BF)
    spread = dot(member, counts.astype(F32).reshape(groups, block_rows).astype(BF))
    here = lax.broadcasted_iota(jnp.int32, (rows, block_rows), 0) % block_rows
    here = here == lax.broadcasted_iota(jnp.int32, (rows, block_rows), 1)
    per_row = jnp.sum(jnp.where(here, spread, 0.0), axis=1, keepdims=True)
    own = sums[:, :, 0].reshape(rows, depth).astype(BF)
    mean = (sums[:, :, 1].reshape(rows, depth) / per_row).astype(BF)
    parts_ref[:, :depth] = own
    parts_ref[:, depth:] = mean
    pre_ref[:rows, :] = (dot(own, weights_v[0]) + dot(mean, weights_v[1])).astype(BF)

    lane = lax.broadcasted_iota(jnp.int32, (1, width), 1)
    valid = seed_count[0, 0, 0]
    marks = jnp.where(lane == block_rows, valid.astype(F32), 0.0)
    for j in range(seed_hops.shape[3]):
        marks = marks + jnp.where((lane == seed_s[0, 0, 0, j]) & (j < valid), 1.0, 0.0)
    target = labels_v[0, 0].astype(F32)
    marks = jnp.concatenate([marks[:, :labels_at], target, marks[:, labels_at + target.shape[1] :]], axis=1)
    meta_rows = pre_ref.shape[0] - rows
    slot_row = lax.broadcasted_iota(jnp.int32, (meta_rows, width), 0) == lax.axis_index("col")
    pre_ref[rows:, :] = jnp.where(slot_row, marks, 0.0).astype(BF)


def upper_kernel(
    batches, block_rows, labels_at, w_two, w_three, *refs
):
    *terms, hidden_ref, loss_ref, pack_ref, hidden_f32 = refs
    rows, width = pack_ref.shape[0] - 6 * batches, pack_ref.shape[1]
    me = lax.axis_index("col")
    label_count = w_three.shape[0]
    pre_one = add_up([term[:rows, :] for term in terms])
    meta = add_up([term[rows:, :] for term in terms])[:batches]
    sig_one = jax.nn.sigmoid(pre_one)
    hidden = (pre_one * sig_one).astype(BF)
    hidden_f32[...] = hidden.astype(F32)
    hidden_ref[...] = hidden_f32[pl.ds(pl.multiple_of(me * block_rows, block_rows), block_rows), :].astype(BF)
    counts = meta[:, block_rows : block_rows + 1]
    target = meta[:, labels_at : labels_at + label_count]
    batch = lax.broadcasted_iota(jnp.int32, (batches, rows), 0)
    row = lax.broadcasted_iota(jnp.int32, (batches, rows), 1)
    tiled = jnp.concatenate([meta[:, :block_rows]] * batches, axis=1)
    adjacency = jnp.where(row // block_rows == batch, tiled, 0.0)
    first = jnp.where(row == batch * block_rows, 1.0, 0.0)
    seeds = dot(first.astype(BF), hidden).astype(BF)
    mean_two = (dot(adjacency.astype(BF), hidden) / counts).astype(BF)
    pre_two = dot(seeds, w_two[0]) + dot(mean_two, w_two[1])
    sig_two = jax.nn.sigmoid(pre_two)
    hidden_two = (pre_two * sig_two).astype(BF)
    logits = dot(hidden_two, w_three[...], NT)
    soft = jnp.maximum(logits, 0.0) + jnp.log1p(jnp.exp(-jnp.abs(logits)))
    losses = jnp.mean(soft - target * logits, axis=1, keepdims=True)
    chosen = lax.broadcasted_iota(jnp.int32, losses.shape, 0) == me
    loss_ref[...] = jnp.sum(jnp.where(chosen, losses, 0.0), axis=0, keepdims=True)
    grad_logits = (jax.nn.sigmoid(logits) - target).astype(BF)
    back_two = dot(grad_logits, w_three[...])
    grad_two = (back_two * silu_slope(pre_two, sig_two)).astype(BF)
    to_seeds = dot(grad_two, w_two[0], NT)
    to_means = dot(grad_two, w_two[1], NT) / counts
    grad_hidden = lax.dot_general(
        jnp.concatenate([adjacency, first], axis=0),
        jnp.concatenate([to_means, to_seeds], axis=0),
        TN,
        precision=lax.Precision.HIGHEST,
        preferred_element_type=F32,
    )
    pack_ref[:rows, :] = (grad_hidden * silu_slope(pre_one, sig_one)).astype(BF)
    blank = jnp.zeros((batches, width - label_count), F32)
    tail = jnp.concatenate(
        [
            seeds.astype(F32),
            mean_two.astype(F32),
            grad_two.astype(F32),
            hidden_two.astype(F32),
            jnp.concatenate([grad_logits.astype(F32), blank], axis=1),
            jnp.zeros((batches, width), F32),
        ],
        axis=0,
    )
    pack_ref[rows:, :] = tail.astype(BF)


def final_kernel(batches, parts_a, pack_a, parts_b, pack_b, one_ref, two_ref, three_ref):
    rows = parts_a.shape[0]
    depth = one_ref.shape[1]

    def part(pack, k):
        if batches % 16 == 0:
            return pack[rows + k * batches : rows + (k + 1) * batches, :]
        return pack[rows:, :].astype(F32)[k * batches : (k + 1) * batches].astype(BF)

    def both(k, m):
        return dot(part(pack_a, k), part(pack_a, m), TN) + dot(part(pack_b, k), part(pack_b, m), TN)

    one = dot(parts_a[...], pack_a[:rows, :], TN) + dot(parts_b[...], pack_b[:rows, :], TN)
    one_ref[0] = one[:depth]
    one_ref[1] = one[depth:]
    two_ref[0] = both(0, 2)
    two_ref[1] = both(1, 2)
    three_ref[...] = both(4, 3)[: three_ref.shape[0], :]


def per_device(
    features,
    block_nodes,
    hop_two,
    hop_two_count,
    hop_one,
    hop_one_count,
    labels,
    weight_one,
    weight_two,
    weight_three,
):
    groups = lax.axis_size("col")
    depth, nodes = features.shape
    width = weight_one.shape[2]
    block_rows = block_nodes.shape[2]
    fan = hop_two.shape[2]
    label_count = weight_three.shape[1]
    rows = groups * block_rows
    meta_rows = -(-groups // 16) * 16
    labels_at = width // 2
    chunks, slots = 16, 8
    mib = 2**20
    row_bytes = rows * width * 4

    parts, pre = pl.pallas_call(
        functools.partial(gather_kernel, chunks, 256, 16, labels_at),
        out_shape=(
            jax.ShapeDtypeStruct((rows, 2 * depth), BF),
            jax.ShapeDtypeStruct((rows + meta_rows, width), BF),
        ),
        in_specs=[HBM] * 7 + [SMEM],
        out_specs=(VMEM, VMEM),
        scratch_shapes=[
            pltpu.VMEM((slots, depth, nodes // chunks), BF),
            pltpu.VMEM((nodes + 8, depth), F32),
            pltpu.VMEM((groups, block_rows // 8, 2, 8, depth), F32),
            pltpu.SMEM((groups, 1, block_rows), jnp.int32),
            pltpu.VMEM((groups, fan, 1, block_rows), jnp.int32),
            pltpu.SMEM((groups, fan, 1, block_rows), jnp.int32),
            pltpu.VMEM((groups, 1, block_rows), jnp.int32),
            pltpu.SMEM((1, 1, 1, hop_one.shape[2]), jnp.int32),
            pltpu.VMEM((1, 1, 1, label_count), jnp.int32),
            pltpu.VMEM(weight_one.shape, BF),
            pltpu.SemaphoreType.DMA((slots,)),
            pltpu.SemaphoreType.DMA((8,)),
        ],
        compiler_params=pltpu.CompilerParams(vmem_limit_bytes=44 * mib + 2 * row_bytes),
    )(
        *(
            pltpu.with_memory_space_constraint(array, pltpu.HBM)
            for array in (
                block_nodes,
                jnp.transpose(hop_two, (0, 2, 1, 3)),
                hop_two_count,
                jnp.transpose(hop_one, (0, 1, 3, 2)),
                labels,
                weight_one,
                features,
            )
        ),
        hop_one_count,
    )

    swap = [(0, 1), (1, 0)]
    parts_b = lax.ppermute(parts, "sub", swap)
    terms = [pre]
    for number, masks in enumerate(phases(groups)):
        pre = add_up(terms).astype(BF) if number else pre
        terms = [pre] + [lax.ppermute(pre, "col", [(i, i ^ m) for i in range(groups)]) for m in masks]
        if number == 0:
            *terms, parts_b = lax.optimization_barrier((*terms, parts_b))

    hidden, loss, pack = pl.pallas_call(
        functools.partial(upper_kernel, groups, block_rows, labels_at),
        out_shape=(
            jax.ShapeDtypeStruct((block_rows, width), BF),
            jax.ShapeDtypeStruct((1, 1), F32),
            jax.ShapeDtypeStruct((rows + 6 * groups, width), BF),
        ),
        in_specs=[VMEM] * (len(terms) + 2),
        out_specs=(VMEM, VMEM, VMEM),
        scratch_shapes=[pltpu.VMEM((rows, width), F32)],
        compiler_params=pltpu.CompilerParams(vmem_limit_bytes=6 * mib + 8 * row_bytes),
    )(weight_two, weight_three.T, *terms)

    pack_b = lax.ppermute(pack, "sub", swap)
    grad_one, grad_two, grad_three = pl.pallas_call(
        functools.partial(final_kernel, groups),
        out_shape=(
            jax.ShapeDtypeStruct((2, depth, width), F32),
            jax.ShapeDtypeStruct((2, width, width), F32),
            jax.ShapeDtypeStruct((label_count, width), F32),
        ),
        in_specs=[VMEM] * 4,
        out_specs=(VMEM, VMEM, VMEM),
        compiler_params=pltpu.CompilerParams(vmem_limit_bytes=6 * mib + 4 * row_bytes),
    )(parts, pack, parts_b, pack_b)
    return (
        hidden.reshape(1, 1, block_rows, width),
        loss,
        grad_one,
        grad_two,
        grad_three.T,
    )


def solution(mesh):
    return jax.shard_map(
        per_device,
        mesh=mesh,
        in_specs=(
            P("col", "grp"),
            P("grp", "sub", None),
            P("grp", "sub", None, None),
            P("grp", "sub", None),
            P(("grp", "col"), "sub", None, None),
            P(("grp", "col"), "sub", None),
            P(("grp", "col"), "sub", None, None),
            P(None, "col", None),
            P(),
            P(),
        ),
        out_specs=(
            P(("grp", "col"), "sub", None, None),
            P(("grp", "col"), "sub"),
            P("grp", "col", None),
            P("grp", None, None),
            P("grp", None),
        ),
        check_vma=False,
    )
```

time: 51.7 us -> 34.3 us (0.66)
  local copies, waits for them, and re-layouts: 8.66 us -> 0.01 us
  other arithmetic: 5.26 us -> 0.04 us
  Pallas kernels: 16.4 us -> 12.9 us
  starting transfers between devices: 8.31 us -> 9.35 us
  waiting for transfers between devices: 11.2 us -> 10.5 us
    unnamed x14 -> x4, local copies, waits for them, and re-layouts: 4.3 us -> 0.01 us
    pallas_call x3, Pallas kernels: 16.4 us -> 12.9 us  [the longest x1 9.82 us: per_device(): pl.pallas_call(functools.partial(gather_kernel, chunks, 256, 16, labels_a...]
    convert_element_type x5 -> x1, other arithmetic: 3.02 us -> 0.04 us  [per_device(): pre = add_up(terms).astype(BF) if number else pre]
    reshape x2 -> x0, local copies, waits for them, and re-layouts: 2.12 us -> none  [the longest x1 1.32 us: per_device(): lax.dynamic_slice_in_dim(hidden, me * block_rows, block_rows, 0)]
    ppermute x5, waiting for transfers between devices: 11.1 us -> 9.1 us  [the longest x4 7.76 us: per_device(): lax.ppermute(pre, 'col', [(i, i ^ m) for i in range(groups)])]
    ppermute x1, waiting for transfers between devices: 0.01 us -> 1.38 us  [per_device(): pack_b = lax.ppermute(pack, 'sub', swap)]
    dynamic_slice x1 -> x0, local copies, waits for them, and re-layouts: 1.2 us -> none  [per_device(): lax.dynamic_slice_in_dim(loss, me, 1, 0)]
    ppermute x5, starting transfers between devices: 8.31 us -> 9.34 us  [the longest x4 9.34 us: per_device(): lax.ppermute(pre, 'col', [(i, i ^ m) for i in range(groups)])]
  transfers between devices with their start and end apart: 6 -> 6, of which waited for: 3 -> 6; matrix products, arithmetic and copies ran while one was open for 6% -> 0% of each run, Pallas kernels for 0% -> 0%
where the time goes in v2:
time: 34.3 us; the launch traced here: 34.1 us
  Pallas kernels  12.9 us (38%)
  waiting for transfers between devices  10.5 us (31%)
  starting transfers between devices  9.35 us (27%)
  between operations  1.36 us (4%)
    pallas_call x1, Pallas kernels, per_device(): pl.pallas_call(functools.partial(gather_kernel, chunks, 256, 16, labels_a...  9.82 us
    ppermute x4, starting transfers between devices, per_device(): lax.ppermute(pre, 'col', [(i, i ^ m) for i in range(groups)])  9.34 us
    ppermute x4, waiting for transfers between devices, per_device(): lax.ppermute(pre, 'col', [(i, i ^ m) for i in range(groups)])  7.76 us
    pallas_call x1, Pallas kernels, per_device(): pl.pallas_call(functools.partial(upper_kernel, groups, block_rows, labels...  1.77 us
    ppermute x1, waiting for transfers between devices, per_device(): pack_b = lax.ppermute(pack, 'sub', swap)  1.38 us
    ppermute x1, waiting for transfers between devices, per_device(): parts_b = lax.ppermute(parts, 'sub', swap)  1.35 us
    pallas_call x1, Pallas kernels, per_device(): pl.pallas_call(functools.partial(final_kernel, groups), out_shape=(jax.Sh...  1.28 us
  transfers between devices with their start and end apart: 6, of which 6 were waited for; matrix products, arithmetic and copies ran while one was open for 0% of the time, Pallas kernels for 0%

profile of v2, /device:TPU:0, one launch (start us, length us, event | category | flops | bytes accessed | tf_op | source)
XLA Modules:
  0.0 34.1 jit_solution(14832904131258143815)
XLA Ops:
  0.6 0.0 copy-start.1
  0.6 0.0 copy-start
  1.3 9.8 %shard_map.137 = (bf16[256,256]{1,0:T(8,128)(2,1)S(1)}, bf16[272,256]{1,0:T(8,128)(2,1)S(1)}) custom-call(s32[8,1,32]{2,1,0:T(1,128)} %own_ids.1, s32[8,10,1,32]{3,2,1,0:T(1,128)} %bitcast.6, s32[8,1,32]{2,1,0:T(1,128)} %hop_counts.1, s32[1,1,1,25]{3,2,1,0:T(1,128)} %bitcast.7, s32[1,1,1,112]{3,2,1,0:T(1,128)} %labels.1, bf16[2,128,256]{2,1,0:T(8,128)(2,1)} %weights.1, ...), custom_call_target="tpu_custom_call" | custom-call | tf_op jit(solution)/shard_map/pallas_call | solution.py:258
  11.2 5.1 %collective-permute-start = (bf16[272,256]{1,0:T(8,128)(2,1)S(1)}, bf16[272,256]{1,0:T(8,128)(2,1)S(1)}, u32[]{:S(2)}, u32[]{:S(2)}) collective-permute-start(bf16[272,256]{1,0:T(8,128)(2,1)S(1)} %get-tuple-element.18), channel_id=1, source_target_pairs={{0,12},{2,14},{4,8},{6,10},{8,4},{10,6},{12,0},{14,2},{1,13},{3,15... | collective-permute-start | bytes 417800 | tf_op jit(solution)/shard_map/ppermute | solution.py:302
  16.3 0.0 collective-permute-start.1
  16.3 1.3 %collective-permute-done.1.parts_b = bf16[256,256]{1,0:T(8,128)(2,1)S(1)} collective-permute-done((bf16[256,256]{1,0:T(8,128)(2,1)S(1)}, bf16[256,256]{1,0:T(8,128)(2,1)S(1)}, u32[]{:S(2)}, u32[]{:S(2)}) %collective-permute-start.1) | collective-permute-done | bytes 131104 | tf_op jit(solution)/shard_map/ppermute | solution.py:298
  17.6 2.4 %collective-permute-done = bf16[272,256]{1,0:T(8,128)(2,1)S(1)} collective-permute-done((bf16[272,256]{1,0:T(8,128)(2,1)S(1)}, bf16[272,256]{1,0:T(8,128)(2,1)S(1)}, u32[]{:S(2)}, u32[]{:S(2)}) %collective-permute-start) | collective-permute-done | bytes 139296 | tf_op jit(solution)/shard_map/ppermute | solution.py:302
  20.1 3.6 %collective-permute-start.4 = (bf16[272,256]{1,0:T(8,128)(2,1)S(1)}, bf16[272,256]{1,0:T(8,128)(2,1)S(1)}, u32[]{:S(2)}, u32[]{:S(2)}) collective-permute-start(bf16[272,256]{1,0:T(8,128)(2,1)S(1)} %add_convert_fusion.refs_0_), channel_id=1, source_target_pairs={{0,6},{2,4},{4,2},{6,0},{8,14},{10,12},{12,10},{14,8},{1,7},{3,5},... | collective-permute-start | bytes 417800 | tf_op jit(solution)/shard_map/ppermute | solution.py:302
  23.7 0.0 collective-permute-start.3
  23.7 0.6 %collective-permute-start.2 = (bf16[272,256]{1,0:T(8,128)(2,1)S(1)}, bf16[272,256]{1,0:T(8,128)(2,1)S(1)}, u32[]{:S(2)}, u32[]{:S(2)}) collective-permute-start(bf16[272,256]{1,0:T(8,128)(2,1)S(1)} %add_convert_fusion.refs_0_), channel_id=1, source_target_pairs={{0,2},{2,0},{4,6},{6,4},{8,10},{10,8},{12,14},{14,12},{1,3},{3,1},... | collective-permute-start | bytes 417800 | tf_op jit(solution)/shard_map/ppermute | solution.py:302
  24.3 3.8 %collective-permute-done.4.refs_3_ = bf16[272,256]{1,0:T(8,128)(2,1)S(1)} collective-permute-done((bf16[272,256]{1,0:T(8,128)(2,1)S(1)}, bf16[272,256]{1,0:T(8,128)(2,1)S(1)}, u32[]{:S(2)}, u32[]{:S(2)}) %collective-permute-start.4) | collective-permute-done | bytes 139296 | tf_op jit(solution)/shard_map/ppermute | solution.py:302
  28.2 1.0 %collective-permute-done.3.refs_2_ = bf16[272,256]{1,0:T(8,128)(2,1)S(1)} collective-permute-done((bf16[272,256]{1,0:T(8,128)(2,1)S(1)}, bf16[272,256]{1,0:T(8,128)(2,1)S(1)}, u32[]{:S(2)}, u32[]{:S(2)}) %collective-permute-start.3) | collective-permute-done | bytes 139296 | tf_op jit(solution)/shard_map/ppermute | solution.py:302
  29.1 0.5 %collective-permute-done.2.refs_1_ = bf16[272,256]{1,0:T(8,128)(2,1)S(1)} collective-permute-done((bf16[272,256]{1,0:T(8,128)(2,1)S(1)}, bf16[272,256]{1,0:T(8,128)(2,1)S(1)}, u32[]{:S(2)}, u32[]{:S(2)}) %collective-permute-start.2) | collective-permute-done | bytes 139296 | tf_op jit(solution)/shard_map/ppermute | solution.py:302
  29.7 0.0 copy-done.1
  29.7 0.0 copy-done
  29.7 1.8 %shard_map.138 = (bf16[32,256]{1,0:T(8,128)(2,1)}, f32[1,1]{1,0:T(1,128)}, bf16[304,256]{1,0:T(8,128)(2,1)S(1)}) custom-call(bf16[2,256,256]{2,1,0:T(8,128)(2,1)S(1)} %copy-done, bf16[112,256]{1,0:T(8,128)(2,1)S(1)} %bitcast.5, bf16[272,256]{1,0:T(8,128)(2,1)S(1)} %add_convert_fusion.refs_0_, bf16[272,256]{1,0:T(8,128)(2,1)S(1)} %collective-permute-done.2.refs_1_, ...), custom_call_target="tpu_custom_call" | custom-call | tf_op jit(solution)/shard_map/pallas_call | solution.py:306
  31.4 0.0 collective-permute-start.5
  31.4 1.4 %collective-permute-done.5.pack_b = bf16[304,256]{1,0:T(8,128)(2,1)S(1)} collective-permute-done((bf16[304,256]{1,0:T(8,128)(2,1)S(1)}, bf16[304,256]{1,0:T(8,128)(2,1)S(1)}, u32[]{:S(2)}, u32[]{:S(2)}) %collective-permute-start.5) | collective-permute-done | bytes 155680 | tf_op jit(solution)/shard_map/ppermute | solution.py:319
  32.8 1.3 %shard_map.139 = (f32[2,128,256]{2,1,0:T(8,128)}, f32[2,256,256]{2,1,0:T(8,128)}, f32[112,256]{1,0:T(8,128)}) custom-call(bf16[256,256]{1,0:T(8,128)(2,1)S(1)} %get-tuple-element.17.parts_a, bf16[304,256]{1,0:T(8,128)(2,1)S(1)} %get-tuple-element.22.pack_a, bf16[256,256]{1,0:T(8,128)(2,1)S(1)} %collective-permute-done.1.parts_b, ...), custom_call_target="tpu_custom_call" | custom-call | tf_op jit(solution)/shard_map/pallas_call | solution.py:320
  (1 shorter events, 0.0 us)
Async XLA Ops:
  0.6 29.0 %copy-start.1 = (bf16[256,112]{0,1:T(8,128)(2,1)S(1)}, bf16[256,112]{0,1:T(8,128)(2,1)}, u32[]{:S(2)}) copy-start(bf16[256,112]{0,1:T(8,128)(2,1)} %param.19) | copy-start | bytes 172036
  0.6 29.0 %copy-start = (bf16[2,256,256]{2,1,0:T(8,128)(2,1)S(1)}, bf16[2,256,256]{2,1,0:T(8,128)(2,1)}, u32[]{:S(2)}) copy-start(bf16[2,256,256]{2,1,0:T(8,128)(2,1)} %w_two.1) | copy-start | bytes 786436
  11.2 8.9 %collective-permute-start = (bf16[272,256]{1,0:T(8,128)(2,1)S(1)}, bf16[272,256]{1,0:T(8,128)(2,1)S(1)}, u32[]{:S(2)}, u32[]{:S(2)}) collective-permute-start(bf16[272,256]{1,0:T(8,128)(2,1)S(1)} %get-tuple-element.18), channel_id=1, source_target_pairs={{0,12},{2,14},{4,8},{6,10},{8,4},{10,6},{12,0},{14,2},{1,13},{3,15... | collective-permute-start | bytes 417800 | tf_op jit(solution)/shard_map/ppermute | solution.py:302
  16.3 1.3 %collective-permute-start.1 = (bf16[256,256]{1,0:T(8,128)(2,1)S(1)}, bf16[256,256]{1,0:T(8,128)(2,1)S(1)}, u32[]{:S(2)}, u32[]{:S(2)}) collective-permute-start(bf16[256,256]{1,0:T(8,128)(2,1)S(1)} %get-tuple-element.17.parts_a), channel_id=1, source_target_pairs={{0,1},{1,0},{2,3},{3,2},{4,5},{5,4},{6,7},{7,6},{8,9},{9,8},{10,11... | collective-permute-start | bytes 393224 | tf_op jit(solution)/shard_map/ppermute | solution.py:298
  20.1 8.1 %collective-permute-start.4 = (bf16[272,256]{1,0:T(8,128)(2,1)S(1)}, bf16[272,256]{1,0:T(8,128)(2,1)S(1)}, u32[]{:S(2)}, u32[]{:S(2)}) collective-permute-start(bf16[272,256]{1,0:T(8,128)(2,1)S(1)} %add_convert_fusion.refs_0_), channel_id=1, source_target_pairs={{0,6},{2,4},{4,2},{6,0},{8,14},{10,12},{12,10},{14,8},{1,7},{3,5},... | collective-permute-start | bytes 417800 | tf_op jit(solution)/shard_map/ppermute | solution.py:302
  23.7 5.4 %collective-permute-start.3 = (bf16[272,256]{1,0:T(8,128)(2,1)S(1)}, bf16[272,256]{1,0:T(8,128)(2,1)S(1)}, u32[]{:S(2)}, u32[]{:S(2)}) collective-permute-start(bf16[272,256]{1,0:T(8,128)(2,1)S(1)} %add_convert_fusion.refs_0_), channel_id=1, source_target_pairs={{0,4},{2,6},{4,0},{6,2},{8,12},{10,14},{12,8},{14,10},{1,5},{3,7},... | collective-permute-start | bytes 417800 | tf_op jit(solution)/shard_map/ppermute | solution.py:302
  23.7 6.0 %collective-permute-start.2 = (bf16[272,256]{1,0:T(8,128)(2,1)S(1)}, bf16[272,256]{1,0:T(8,128)(2,1)S(1)}, u32[]{:S(2)}, u32[]{:S(2)}) collective-permute-start(bf16[272,256]{1,0:T(8,128)(2,1)S(1)} %add_convert_fusion.refs_0_), channel_id=1, source_target_pairs={{0,2},{2,0},{4,6},{6,4},{8,10},{10,8},{12,14},{14,12},{1,3},{3,1},... | collective-permute-start | bytes 417800 | tf_op jit(solution)/shard_map/ppermute | solution.py:302
  31.4 1.4 %collective-permute-start.5 = (bf16[304,256]{1,0:T(8,128)(2,1)S(1)}, bf16[304,256]{1,0:T(8,128)(2,1)S(1)}, u32[]{:S(2)}, u32[]{:S(2)}) collective-permute-start(bf16[304,256]{1,0:T(8,128)(2,1)S(1)} %get-tuple-element.22.pack_a), channel_id=1, source_target_pairs={{0,1},{1,0},{2,3},{3,2},{4,5},{5,4},{6,7},{7,6},{8,9},{9,8},{10,11... | collective-permute-start | bytes 466952 | tf_op jit(solution)/shard_map/ppermute | solution.py:319

commit v3 on v2

--- a/solution.py
+++ b/solution.py
@@ -51,15 +51,15 @@
 ):
     depth, nodes = features.shape
     span = nodes // chunks
-    slots = stage.shape[0]
+    early = 5
     groups, _, block_rows = own_ids.shape
     fan = hop_ids.shape[1]
     rows = groups * block_rows
     width = weights.shape[2]
 
-    def fetch(k, slot):
+    def fetch(k):
         at = pl.multiple_of(k * span, span)
-        return pltpu.make_async_copy(features.at[:, pl.ds(at, span)], stage.at[slot], sems.at[slot])
+        return pltpu.make_async_copy(features.at[:, pl.ds(at, span)], stage.at[k], sems.at[k])
 
     inputs = [
         pltpu.make_async_copy(source, target, small.at[k])
@@ -74,12 +74,11 @@
             )
         )
     ]
-    inputs[0].start()
-    inputs[1].start()
-    for k in range(slots):
-        fetch(k, k).start()
-    for copy in inputs[2:]:
+    for copy in inputs[:-1]:
         copy.start()
+    for k in range(early):
+        fetch(k).start()
+    inputs[-1].start()
     rows_f32[pl.ds(nodes, 8), :] = jnp.zeros((8, depth), F32)
     inputs[0].wait()
     inputs[1].wait()
@@ -88,27 +87,26 @@
     hop_v[...] = jnp.where(slot_of < counts[:, :, None, :], hop_v[...], nodes)
     to_scalars = pltpu.make_async_copy(hop_v, hop_s, small.at[len(inputs)])
     to_scalars.start()
+    for k in range(early, chunks):
+        fetch(k).start()
+
+    eye = jnp.where(lax.broadcasted_iota(jnp.int32, (block, block), 0) == lax.broadcasted_iota(jnp.int32, (block, block), 1), 1.0, 0.0).astype(BF)
 
     def chunk(k, carry):
-        slot = lax.rem(k, slots)
-        fetch(k, slot).wait()
+        fetch(k).wait()
 
         def turn(i, carry):
             for u in range(unroll):
                 at = pl.multiple_of((i * unroll + u) * block, block)
-                part = stage[slot, :, pl.ds(at, block)]
+                part = stage[k, :, pl.ds(at, block)]
                 if depth % 128 == 0:
-                    flipped = part.T.astype(F32)
+                    flipped = part.T.astype(F32) if u % 4 else dot(eye, part, NT)
                 else:
                     flipped = part.astype(F32).T
                 rows_f32[pl.ds(pl.multiple_of(k * span + at, block), block), :] = flipped
             return carry
 
         lax.fori_loop(0, span // block // unroll, turn, 0)
-
-        @pl.when(k + slots < chunks)
-        def _():
-            fetch(k + slots, slot).start()
 
         return carry
 
@@ -127,7 +125,7 @@
             sums[b, g, 1, q : q + 1, :] = total
         return carry
 
-    lax.fori_loop(0, groups, take, 0)
+    lax.fori_loop(0, groups, take, 0, unroll=min(groups, 8))
     member = lax.broadcasted_iota(jnp.int32, (rows, groups), 0) // block_rows
     member = jnp.where(member == lax.broadcasted_iota(jnp.int32, (rows, groups), 1), 1.0, 0.0).astype(BF)
     spread = dot(member, counts.astype(F32).reshape(groups, block_rows).astype(BF))
@@ -172,9 +170,12 @@
     tiled = jnp.concatenate([meta[:, :block_rows]] * batches, axis=1)
     adjacency = jnp.where(row // block_rows == batch, tiled, 0.0)
     first = jnp.where(row == batch * block_rows, 1.0, 0.0)
-    seeds = dot(first.astype(BF), hidden).astype(BF)
-    mean_two = (dot(adjacency.astype(BF), hidden) / counts).astype(BF)
-    pre_two = dot(seeds, w_two[0]) + dot(mean_two, w_two[1])
+    pick = jnp.concatenate([first, adjacency], axis=0).astype(BF)
+    picked = dot(pick, hidden)
+    seeds = picked[:batches].astype(BF)
+    mean_two = (picked[batches:] / counts).astype(BF)
+    w_both = w_two[...].reshape(2 * width, width)
+    pre_two = dot(jnp.concatenate([seeds, mean_two], axis=1), w_both)
     sig_two = jax.nn.sigmoid(pre_two)
     hidden_two = (pre_two * sig_two).astype(BF)
     logits = dot(hidden_two, w_three[...], NT)
@@ -185,15 +186,13 @@
     grad_logits = (jax.nn.sigmoid(logits) - target).astype(BF)
     back_two = dot(grad_logits, w_three[...])
     grad_two = (back_two * silu_slope(pre_two, sig_two)).astype(BF)
-    to_seeds = dot(grad_two, w_two[0], NT)
-    to_means = dot(grad_two, w_two[1], NT) / counts
-    grad_hidden = lax.dot_general(
-        jnp.concatenate([adjacency, first], axis=0),
-        jnp.concatenate([to_means, to_seeds], axis=0),
-        TN,
-        precision=lax.Precision.HIGHEST,
-        preferred_element_type=F32,
-    )
+    back_both = dot(grad_two, w_both, NT)
+    spread = jnp.concatenate([back_both[:, :width], back_both[:, width:] / counts], axis=0)
+    pieces = []
+    for _ in range(3):
+        pieces.append(spread.astype(BF))
+        spread = spread - pieces[-1].astype(F32)
+    grad_hidden = dot(jnp.concatenate([pick] * 3, axis=0), jnp.concatenate(pieces, axis=0), TN)
     pack_ref[:rows, :] = (grad_hidden * silu_slope(pre_one, sig_one)).astype(BF)
     blank = jnp.zeros((batches, width - label_count), F32)
     tail = jnp.concatenate(
@@ -251,7 +250,7 @@
     rows = groups * block_rows
     meta_rows = -(-groups // 16) * 16
     labels_at = width // 2
-    chunks, slots = 16, 8
+    chunks = 16
     mib = 2**20
     row_bytes = rows * width * 4
 
@@ -264,7 +263,7 @@
         in_specs=[HBM] * 7 + [SMEM],
         out_specs=(VMEM, VMEM),
         scratch_shapes=[
-            pltpu.VMEM((slots, depth, nodes // chunks), BF),
+            pltpu.VMEM((chunks, depth, nodes // chunks), BF),
             pltpu.VMEM((nodes + 8, depth), F32),
             pltpu.VMEM((groups, block_rows // 8, 2, 8, depth), F32),
             pltpu.SMEM((groups, 1, block_rows), jnp.int32),
@@ -274,10 +273,10 @@
             pltpu.SMEM((1, 1, 1, hop_one.shape[2]), jnp.int32),
             pltpu.VMEM((1, 1, 1, label_count), jnp.int32),
             pltpu.VMEM(weight_one.shape, BF),
-            pltpu.SemaphoreType.DMA((slots,)),
+            pltpu.SemaphoreType.DMA((chunks,)),
             pltpu.SemaphoreType.DMA((8,)),
         ],
-        compiler_params=pltpu.CompilerParams(vmem_limit_bytes=44 * mib + 2 * row_bytes),
+        compiler_params=pltpu.CompilerParams(vmem_limit_bytes=52 * mib + 2 * row_bytes),
     )(
         *(
             pltpu.with_memory_space_constraint(array, pltpu.HBM)

time: 34.3 us -> 32.5 us (0.948)
  Pallas kernels: 12.9 us -> 11.1 us
    pallas_call x1, Pallas kernels: 9.82 us -> 8.51 us  [per_device(): pl.pallas_call(functools.partial(gather_kernel, chunks, 256, 16, labels_a...]
    pallas_call x1, Pallas kernels: 1.77 us -> 1.34 us  [per_device(): pl.pallas_call(functools.partial(upper_kernel, groups, block_rows, labels...]
where the time goes in v3:
time: 32.5 us; the launch traced here: 32.3 us
  Pallas kernels  11.1 us (34%)
  waiting for transfers between devices  10.4 us (32%)
  starting transfers between devices  9.33 us (29%)
  between operations  1.36 us (4%)
    ppermute x4, starting transfers between devices, per_device(): lax.ppermute(pre, 'col', [(i, i ^ m) for i in range(groups)])  9.33 us
    pallas_call x1, Pallas kernels, per_device(): pl.pallas_call(functools.partial(gather_kernel, chunks, 256, 16, labels_a...  8.51 us
    ppermute x4, waiting for transfers between devices, per_device(): lax.ppermute(pre, 'col', [(i, i ^ m) for i in range(groups)])  7.71 us
    ppermute x1, waiting for transfers between devices, per_device(): pack_b = lax.ppermute(pack, 'sub', swap)  1.38 us
    ppermute x1, waiting for transfers between devices, per_device(): parts_b = lax.ppermute(parts, 'sub', swap)  1.35 us
    pallas_call x1, Pallas kernels, per_device(): pl.pallas_call(functools.partial(upper_kernel, groups, block_rows, labels...  1.34 us
    pallas_call x1, Pallas kernels, per_device(): pl.pallas_call(functools.partial(final_kernel, groups), out_shape=(jax.Sh...  1.28 us
  transfers between devices with their start and end apart: 6, of which 6 were waited for; matrix products, arithmetic and copies ran while one was open for 0% of the time, Pallas kernels for 0%

profile of v3, /device:TPU:0, one launch (start us, length us, event | category | flops | bytes accessed | tf_op | source)
XLA Modules:
  0.0 32.3 jit_solution(10273535967182950018)
XLA Ops:
  0.6 0.0 copy-start.1
  0.6 0.0 copy-start
  1.3 8.5 %shard_map.137 = (bf16[256,256]{1,0:T(8,128)(2,1)S(1)}, bf16[272,256]{1,0:T(8,128)(2,1)S(1)}) custom-call(s32[8,1,32]{2,1,0:T(1,128)} %own_ids.1, s32[8,10,1,32]{3,2,1,0:T(1,128)} %bitcast.6, s32[8,1,32]{2,1,0:T(1,128)} %hop_counts.1, s32[1,1,1,25]{3,2,1,0:T(1,128)} %bitcast.7, s32[1,1,1,112]{3,2,1,0:T(1,128)} %labels.1, bf16[2,128,256]{2,1,0:T(8,128)(2,1)} %weights.1, ...), custom_call_target="tpu_custom_call" | custom-call | tf_op jit(solution)/shard_map/pallas_call | solution.py:257
  9.9 5.1 %collective-permute-start = (bf16[272,256]{1,0:T(8,128)(2,1)S(1)}, bf16[272,256]{1,0:T(8,128)(2,1)S(1)}, u32[]{:S(2)}, u32[]{:S(2)}) collective-permute-start(bf16[272,256]{1,0:T(8,128)(2,1)S(1)} %get-tuple-element.18), channel_id=1, source_target_pairs={{0,12},{2,14},{4,8},{6,10},{8,4},{10,6},{12,0},{14,2},{1,13},{3,15... | collective-permute-start | bytes 417800 | tf_op jit(solution)/shard_map/ppermute | solution.py:301
  15.0 0.0 collective-permute-start.1
  15.0 1.3 %collective-permute-done.1.parts_b = bf16[256,256]{1,0:T(8,128)(2,1)S(1)} collective-permute-done((bf16[256,256]{1,0:T(8,128)(2,1)S(1)}, bf16[256,256]{1,0:T(8,128)(2,1)S(1)}, u32[]{:S(2)}, u32[]{:S(2)}) %collective-permute-start.1) | collective-permute-done | bytes 131104 | tf_op jit(solution)/shard_map/ppermute | solution.py:297
  16.3 2.4 %collective-permute-done = bf16[272,256]{1,0:T(8,128)(2,1)S(1)} collective-permute-done((bf16[272,256]{1,0:T(8,128)(2,1)S(1)}, bf16[272,256]{1,0:T(8,128)(2,1)S(1)}, u32[]{:S(2)}, u32[]{:S(2)}) %collective-permute-start) | collective-permute-done | bytes 139296 | tf_op jit(solution)/shard_map/ppermute | solution.py:301
  18.8 3.6 %collective-permute-start.4 = (bf16[272,256]{1,0:T(8,128)(2,1)S(1)}, bf16[272,256]{1,0:T(8,128)(2,1)S(1)}, u32[]{:S(2)}, u32[]{:S(2)}) collective-permute-start(bf16[272,256]{1,0:T(8,128)(2,1)S(1)} %add_convert_fusion.refs_0_), channel_id=1, source_target_pairs={{0,6},{2,4},{4,2},{6,0},{8,14},{10,12},{12,10},{14,8},{1,7},{3,5},... | collective-permute-start | bytes 417800 | tf_op jit(solution)/shard_map/ppermute | solution.py:301
  22.4 0.0 collective-permute-start.3
  22.4 0.6 %collective-permute-start.2 = (bf16[272,256]{1,0:T(8,128)(2,1)S(1)}, bf16[272,256]{1,0:T(8,128)(2,1)S(1)}, u32[]{:S(2)}, u32[]{:S(2)}) collective-permute-start(bf16[272,256]{1,0:T(8,128)(2,1)S(1)} %add_convert_fusion.refs_0_), channel_id=1, source_target_pairs={{0,2},{2,0},{4,6},{6,4},{8,10},{10,8},{12,14},{14,12},{1,3},{3,1},... | collective-permute-start | bytes 417800 | tf_op jit(solution)/shard_map/ppermute | solution.py:301
  23.0 3.8 %collective-permute-done.4.refs_3_ = bf16[272,256]{1,0:T(8,128)(2,1)S(1)} collective-permute-done((bf16[272,256]{1,0:T(8,128)(2,1)S(1)}, bf16[272,256]{1,0:T(8,128)(2,1)S(1)}, u32[]{:S(2)}, u32[]{:S(2)}) %collective-permute-start.4) | collective-permute-done | bytes 139296 | tf_op jit(solution)/shard_map/ppermute | solution.py:301
  26.8 1.0 %collective-permute-done.3.refs_2_ = bf16[272,256]{1,0:T(8,128)(2,1)S(1)} collective-permute-done((bf16[272,256]{1,0:T(8,128)(2,1)S(1)}, bf16[272,256]{1,0:T(8,128)(2,1)S(1)}, u32[]{:S(2)}, u32[]{:S(2)}) %collective-permute-start.3) | collective-permute-done | bytes 139296 | tf_op jit(solution)/shard_map/ppermute | solution.py:301
  27.8 0.5 %collective-permute-done.2.refs_1_ = bf16[272,256]{1,0:T(8,128)(2,1)S(1)} collective-permute-done((bf16[272,256]{1,0:T(8,128)(2,1)S(1)}, bf16[272,256]{1,0:T(8,128)(2,1)S(1)}, u32[]{:S(2)}, u32[]{:S(2)}) %collective-permute-start.2) | collective-permute-done | bytes 139296 | tf_op jit(solution)/shard_map/ppermute | solution.py:301
  28.3 0.0 copy-done.1
  28.3 0.0 copy-done
  28.3 1.3 %shard_map.138 = (bf16[32,256]{1,0:T(8,128)(2,1)}, f32[1,1]{1,0:T(1,128)}, bf16[304,256]{1,0:T(8,128)(2,1)S(1)}) custom-call(bf16[2,256,256]{2,1,0:T(8,128)(2,1)S(1)} %copy-done, bf16[112,256]{1,0:T(8,128)(2,1)S(1)} %bitcast.5, bf16[272,256]{1,0:T(8,128)(2,1)S(1)} %add_convert_fusion.refs_0_, bf16[272,256]{1,0:T(8,128)(2,1)S(1)} %collective-permute-done.2.refs_1_, ...), custom_call_target="tpu_custom_call" | custom-call | tf_op jit(solution)/shard_map/pallas_call | solution.py:305
  29.6 0.0 collective-permute-start.5
  29.6 1.4 %collective-permute-done.5.pack_b = bf16[304,256]{1,0:T(8,128)(2,1)S(1)} collective-permute-done((bf16[304,256]{1,0:T(8,128)(2,1)S(1)}, bf16[304,256]{1,0:T(8,128)(2,1)S(1)}, u32[]{:S(2)}, u32[]{:S(2)}) %collective-permute-start.5) | collective-permute-done | bytes 155680 | tf_op jit(solution)/shard_map/ppermute | solution.py:318
  31.0 1.3 %shard_map.139 = (f32[2,128,256]{2,1,0:T(8,128)}, f32[2,256,256]{2,1,0:T(8,128)}, f32[112,256]{1,0:T(8,128)}) custom-call(bf16[256,256]{1,0:T(8,128)(2,1)S(1)} %get-tuple-element.17.parts_a, bf16[304,256]{1,0:T(8,128)(2,1)S(1)} %get-tuple-element.22.pack_a, bf16[256,256]{1,0:T(8,128)(2,1)S(1)} %collective-permute-done.1.parts_b, ...), custom_call_target="tpu_custom_call" | custom-call | tf_op jit(solution)/shard_map/pallas_call | solution.py:319
  (1 shorter events, 0.0 us)
Async XLA Ops:
  0.6 27.7 %copy-start.1 = (bf16[256,112]{0,1:T(8,128)(2,1)S(1)}, bf16[256,112]{0,1:T(8,128)(2,1)}, u32[]{:S(2)}) copy-start(bf16[256,112]{0,1:T(8,128)(2,1)} %param.19) | copy-start | bytes 172036
  0.6 27.7 %copy-start = (bf16[2,256,256]{2,1,0:T(8,128)(2,1)S(1)}, bf16[2,256,256]{2,1,0:T(8,128)(2,1)}, u32[]{:S(2)}) copy-start(bf16[2,256,256]{2,1,0:T(8,128)(2,1)} %w_two.1) | copy-start | bytes 786436
  9.9 8.9 %collective-permute-start = (bf16[272,256]{1,0:T(8,128)(2,1)S(1)}, bf16[272,256]{1,0:T(8,128)(2,1)S(1)}, u32[]{:S(2)}, u32[]{:S(2)}) collective-permute-start(bf16[272,256]{1,0:T(8,128)(2,1)S(1)} %get-tuple-element.18), channel_id=1, source_target_pairs={{0,12},{2,14},{4,8},{6,10},{8,4},{10,6},{12,0},{14,2},{1,13},{3,15... | collective-permute-start | bytes 417800 | tf_op jit(solution)/shard_map/ppermute | solution.py:301
  15.0 1.3 %collective-permute-start.1 = (bf16[256,256]{1,0:T(8,128)(2,1)S(1)}, bf16[256,256]{1,0:T(8,128)(2,1)S(1)}, u32[]{:S(2)}, u32[]{:S(2)}) collective-permute-start(bf16[256,256]{1,0:T(8,128)(2,1)S(1)} %get-tuple-element.17.parts_a), channel_id=1, source_target_pairs={{0,1},{1,0},{2,3},{3,2},{4,5},{5,4},{6,7},{7,6},{8,9},{9,8},{10,11... | collective-permute-start | bytes 393224 | tf_op jit(solution)/shard_map/ppermute | solution.py:297
  18.8 8.0 %collective-permute-start.4 = (bf16[272,256]{1,0:T(8,128)(2,1)S(1)}, bf16[272,256]{1,0:T(8,128)(2,1)S(1)}, u32[]{:S(2)}, u32[]{:S(2)}) collective-permute-start(bf16[272,256]{1,0:T(8,128)(2,1)S(1)} %add_convert_fusion.refs_0_), channel_id=1, source_target_pairs={{0,6},{2,4},{4,2},{6,0},{8,14},{10,12},{12,10},{14,8},{1,7},{3,5},... | collective-permute-start | bytes 417800 | tf_op jit(solution)/shard_map/ppermute | solution.py:301
  22.4 5.5 %collective-permute-start.3 = (bf16[272,256]{1,0:T(8,128)(2,1)S(1)}, bf16[272,256]{1,0:T(8,128)(2,1)S(1)}, u32[]{:S(2)}, u32[]{:S(2)}) collective-permute-start(bf16[272,256]{1,0:T(8,128)(2,1)S(1)} %add_convert_fusion.refs_0_), channel_id=1, source_target_pairs={{0,4},{2,6},{4,0},{6,2},{8,12},{10,14},{12,8},{14,10},{1,5},{3,7},... | collective-permute-start | bytes 417800 | tf_op jit(solution)/shard_map/ppermute | solution.py:301
  22.4 5.9 %collective-permute-start.2 = (bf16[272,256]{1,0:T(8,128)(2,1)S(1)}, bf16[272,256]{1,0:T(8,128)(2,1)S(1)}, u32[]{:S(2)}, u32[]{:S(2)}) collective-permute-start(bf16[272,256]{1,0:T(8,128)(2,1)S(1)} %add_convert_fusion.refs_0_), channel_id=1, source_target_pairs={{0,2},{2,0},{4,6},{6,4},{8,10},{10,8},{12,14},{14,12},{1,3},{3,1},... | collective-permute-start | bytes 417800 | tf_op jit(solution)/shard_map/ppermute | solution.py:301
  29.6 1.4 %collective-permute-start.5 = (bf16[304,256]{1,0:T(8,128)(2,1)S(1)}, bf16[304,256]{1,0:T(8,128)(2,1)S(1)}, u32[]{:S(2)}, u32[]{:S(2)}) collective-permute-start(bf16[304,256]{1,0:T(8,128)(2,1)S(1)} %get-tuple-element.22.pack_a), channel_id=1, source_target_pairs={{0,1},{1,0},{2,3},{3,2},{4,5},{5,4},{6,7},{7,6},{8,9},{9,8},{10,11... | collective-permute-start | bytes 466952 | tf_op jit(solution)/shard_map/ppermute | solution.py:318

commit v4 on v3

--- a/solution.py
+++ b/solution.py
@@ -46,7 +46,7 @@
 
 def gather_kernel(
     chunks, block, unroll, labels_at, own_ids, hop_ids, hop_counts, seed_hops, labels, weights, features,
-    seed_count, parts_ref, pre_ref, stage, rows_f32, sums, own_s, hop_v, hop_s, count_v, seed_s, labels_v, weights_v,
+    seed_count, parts_ref, pre_ref, stage, rows_f32, sums, count_rows, own_s, hop_v, hop_s, count_v, seed_s, labels_v, weights_v,
     sems, small,
 ):
     depth, nodes = features.shape
@@ -90,6 +90,26 @@
     for k in range(early, chunks):
         fetch(k).start()
 
+    member = lax.broadcasted_iota(jnp.int32, (rows, groups), 0) // block_rows
+    member = jnp.where(member == lax.broadcasted_iota(jnp.int32, (rows, groups), 1), 1.0, 0.0).astype(BF)
+    spread = dot(member, counts.astype(F32).reshape(groups, block_rows).astype(BF))
+    here = lax.broadcasted_iota(jnp.int32, (rows, block_rows), 0) % block_rows
+    here = here == lax.broadcasted_iota(jnp.int32, (rows, block_rows), 1)
+    per_row = jnp.sum(jnp.where(here, spread, 0.0), axis=1, keepdims=True)
+    count_rows[...] = jnp.broadcast_to(per_row, count_rows.shape)
+    for copy in inputs[3:5]:
+        copy.wait()
+    lane = lax.broadcasted_iota(jnp.int32, (1, width), 1)
+    valid = seed_count[0, 0, 0]
+    marks = jnp.where(lane == block_rows, valid.astype(F32), 0.0)
+    for j in range(seed_hops.shape[3]):
+        marks = marks + jnp.where((lane == seed_s[0, 0, 0, j]) & (j < valid), 1.0, 0.0)
+    target = labels_v[0, 0].astype(F32)
+    marks = jnp.concatenate([marks[:, :labels_at], target, marks[:, labels_at + target.shape[1] :]], axis=1)
+    meta_rows = pre_ref.shape[0] - rows
+    slot_row = lax.broadcasted_iota(jnp.int32, (meta_rows, width), 0) == lax.axis_index("col")
+    pre_ref[rows:, :] = jnp.where(slot_row, marks, 0.0).astype(BF)
+
     eye = jnp.where(lax.broadcasted_iota(jnp.int32, (block, block), 0) == lax.broadcasted_iota(jnp.int32, (block, block), 1), 1.0, 0.0).astype(BF)
 
     def chunk(k, carry):
@@ -111,43 +131,38 @@
         return carry
 
     lax.fori_loop(0, chunks, chunk, 0)
-    for copy in inputs[2:]:
-        copy.wait()
+    inputs[2].wait()
+    inputs[5].wait()
     to_scalars.wait()
 
-    def take(b, carry):
-        for r in range(block_rows):
-            g, q = r // 8, r % 8
-            sums[b, g, 0, q : q + 1, :] = rows_f32[pl.ds(own_s[b, 0, r], 1), :]
-            total = rows_f32[pl.ds(hop_s[b, 0, 0, r], 1), :]
-            for j in range(1, fan):
-                total = total + rows_f32[pl.ds(hop_s[b, j, 0, r], 1), :]
-            sums[b, g, 1, q : q + 1, :] = total
-        return carry
-
-    lax.fori_loop(0, groups, take, 0, unroll=min(groups, 8))
-    member = lax.broadcasted_iota(jnp.int32, (rows, groups), 0) // block_rows
-    member = jnp.where(member == lax.broadcasted_iota(jnp.int32, (rows, groups), 1), 1.0, 0.0).astype(BF)
-    spread = dot(member, counts.astype(F32).reshape(groups, block_rows).astype(BF))
-    here = lax.broadcasted_iota(jnp.int32, (rows, block_rows), 0) % block_rows
-    here = here == lax.broadcasted_iota(jnp.int32, (rows, block_rows), 1)
-    per_row = jnp.sum(jnp.where(here, spread, 0.0), axis=1, keepdims=True)
-    own = sums[:, :, 0].reshape(rows, depth).astype(BF)
-    mean = (sums[:, :, 1].reshape(rows, depth) / per_row).astype(BF)
-    parts_ref[:, :depth] = own
-    parts_ref[:, depth:] = mean
-    pre_ref[:rows, :] = (dot(own, weights_v[0]) + dot(mean, weights_v[1])).astype(BF)
-
-    lane = lax.broadcasted_iota(jnp.int32, (1, width), 1)
-    valid = seed_count[0, 0, 0]
-    marks = jnp.where(lane == block_rows, valid.astype(F32), 0.0)
-    for j in range(seed_hops.shape[3]):
-        marks = marks + jnp.where((lane == seed_s[0, 0, 0, j]) & (j < valid), 1.0, 0.0)
-    target = labels_v[0, 0].astype(F32)
-    marks = jnp.concatenate([marks[:, :labels_at], target, marks[:, labels_at + target.shape[1] :]], axis=1)
-    meta_rows = pre_ref.shape[0] - rows
-    slot_row = lax.broadcasted_iota(jnp.int32, (meta_rows, width), 0) == lax.axis_index("col")
-    pre_ref[rows:, :] = jnp.where(slot_row, marks, 0.0).astype(BF)
+    w_both = weights_v[...].reshape(2 * depth, width)
+
+    def take(first, several):
+        for b in range(several):
+            b = first + b
+            for r in range(block_rows):
+                g, q = r // 8, r % 8
+                sums[b, g, 0, q : q + 1, :] = rows_f32[pl.ds(own_s[b, 0, r], 1), :]
+                total = rows_f32[pl.ds(hop_s[b, 0, 0, r], 1), :]
+                for j in range(1, fan):
+                    total = total + rows_f32[pl.ds(hop_s[b, j, 0, r], 1), :]
+                sums[b, g, 1, q : q + 1, :] = total
+        size = several * block_rows
+        here = pl.ds(first * block_rows, size)
+        parts_ref[here, :depth] = sums[pl.ds(first, several), :, 0].reshape(size, depth).astype(BF)
+        mean = sums[pl.ds(first, several), :, 1].reshape(size, depth) / count_rows[here, :]
+        parts_ref[here, depth:] = mean.astype(BF)
+        pre_ref[here, :] = dot(parts_ref[here, :], w_both).astype(BF)
+
+    several = min(groups, 4)
+    if groups <= 8:
+        for first in range(0, groups, several):
+            take(first, several)
+    else:
+
+        @pl.loop(0, groups // several)
+        def _(turn):
+            take(turn * several, several)
 
 
 def upper_kernel(
@@ -209,24 +224,36 @@
     pack_ref[rows:, :] = tail.astype(BF)
 
 
-def final_kernel(batches, parts_a, pack_a, parts_b, pack_b, one_ref, two_ref, three_ref):
-    rows = parts_a.shape[0]
-    depth = one_ref.shape[1]
-
-    def part(pack, k):
+def products(batches, parts_t, pack):
+    rows = parts_t.shape[1]
+
+    def part(k):
         if batches % 16 == 0:
             return pack[rows + k * batches : rows + (k + 1) * batches, :]
         return pack[rows:, :].astype(F32)[k * batches : (k + 1) * batches].astype(BF)
 
-    def both(k, m):
-        return dot(part(pack_a, k), part(pack_a, m), TN) + dot(part(pack_b, k), part(pack_b, m), TN)
-
-    one = dot(parts_a[...], pack_a[:rows, :], TN) + dot(parts_b[...], pack_b[:rows, :], TN)
+    one = dot(parts_t, pack[:rows, :])
+    return one, dot(part(0), part(2), TN), dot(part(1), part(2), TN), dot(part(4), part(3), TN)
+
+
+def half_kernel(batches, parts_a, pack_a, parts_b, one_ref, two_ref, three_ref, flipped_ref):
+    one, seeds, means, three = products(batches, parts_a[...].T, pack_a)
+    one_ref[...] = one
+    two_ref[0] = seeds
+    two_ref[1] = means
+    three_ref[...] = three
+    flipped_ref[...] = parts_b[...].T
+
+
+def final_kernel(batches, flipped, pack_b, one_a, two_a, three_a, one_ref, two_ref, three_ref):
+    depth = one_ref.shape[1]
+    one, seeds, means, three = products(batches, flipped[...], pack_b)
+    one = one_a[...] + one
     one_ref[0] = one[:depth]
     one_ref[1] = one[depth:]
-    two_ref[0] = both(0, 2)
-    two_ref[1] = both(1, 2)
-    three_ref[...] = both(4, 3)[: three_ref.shape[0], :]
+    two_ref[0] = two_a[0] + seeds
+    two_ref[1] = two_a[1] + means
+    three_ref[...] = (three_a[...] + three)[: three_ref.shape[0], :]
 
 
 def per_device(
@@ -266,6 +293,7 @@
             pltpu.VMEM((chunks, depth, nodes // chunks), BF),
             pltpu.VMEM((nodes + 8, depth), F32),
             pltpu.VMEM((groups, block_rows // 8, 2, 8, depth), F32),
+            pltpu.VMEM((rows, depth), F32),
             pltpu.SMEM((groups, 1, block_rows), jnp.int32),
             pltpu.VMEM((groups, fan, 1, block_rows), jnp.int32),
             pltpu.SMEM((groups, fan, 1, block_rows), jnp.int32),
@@ -316,6 +344,18 @@
     )(weight_two, weight_three.T, *terms)
 
     pack_b = lax.ppermute(pack, "sub", swap)
+    one, two, three, flipped_b = pl.pallas_call(
+        functools.partial(half_kernel, groups),
+        out_shape=(
+            jax.ShapeDtypeStruct((2 * depth, width), F32),
+            jax.ShapeDtypeStruct((2, width, width), F32),
+            jax.ShapeDtypeStruct((width, width), F32),
+            jax.ShapeDtypeStruct((2 * depth, rows), BF),
+        ),
+        in_specs=[VMEM] * 3,
+        out_specs=(VMEM,) * 4,
+        compiler_params=pltpu.CompilerParams(vmem_limit_bytes=6 * mib + 4 * row_bytes),
+    )(parts, pack, parts_b)
     grad_one, grad_two, grad_three = pl.pallas_call(
         functools.partial(final_kernel, groups),
         out_shape=(
@@ -323,10 +363,10 @@
             jax.ShapeDtypeStruct((2, width, width), F32),
             jax.ShapeDtypeStruct((label_count, width), F32),
         ),
-        in_specs=[VMEM] * 4,
-        out_specs=(VMEM, VMEM, VMEM),
+        in_specs=[VMEM] * 5,
+        out_specs=(VMEM,) * 3,
         compiler_params=pltpu.CompilerParams(vmem_limit_bytes=6 * mib + 4 * row_bytes),
-    )(parts, pack, parts_b, pack_b)
+    )(flipped_b, pack_b, one, two, three)
     return (
         hidden.reshape(1, 1, block_rows, width),
         loss,

time: 32.5 us -> 32.3 us (level)
    ppermute x1, waiting for transfers between devices: 1.38 us -> 1.05 us  [per_device(): pack_b = lax.ppermute(pack, 'sub', swap)]
  transfers between devices with their start and end apart: 6 -> 6, of which waited for: 6 -> 6; matrix products, arithmetic and copies ran while one was open for 0% -> 0% of each run, Pallas kernels for 0% -> 1%
where the time goes in v4:
time: 32.3 us; the launch traced here: 32.1 us
  Pallas kernels  11.3 us (35%)
  waiting for transfers between devices  10.1 us (31%)
  starting transfers between devices  9.33 us (29%)
  between operations  1.36 us (4%)
    ppermute x4, starting transfers between devices, per_device(): lax.ppermute(pre, 'col', [(i, i ^ m) for i in range(groups)])  9.33 us
    pallas_call x1, Pallas kernels, per_device(): pl.pallas_call(functools.partial(gather_kernel, chunks, 256, 16, labels_a...  8.49 us
    ppermute x4, waiting for transfers between devices, per_device(): lax.ppermute(pre, 'col', [(i, i ^ m) for i in range(groups)])  7.72 us
    ppermute x1, waiting for transfers between devices, per_device(): parts_b = lax.ppermute(parts, 'sub', swap)  1.35 us
    pallas_call x1, Pallas kernels, per_device(): pl.pallas_call(functools.partial(upper_kernel, groups, block_rows, labels...  1.34 us
    pallas_call x1, Pallas kernels, per_device(): pl.pallas_call(functools.partial(final_kernel, groups), out_shape=(jax.Sh...  1.13 us
    ppermute x1, waiting for transfers between devices, per_device(): pack_b = lax.ppermute(pack, 'sub', swap)  1.05 us
  transfers between devices with their start and end apart: 6, of which 6 were waited for; matrix products, arithmetic and copies ran while one was open for 0% of the time, Pallas kernels for 1%

profile of v4, /device:TPU:0, one launch (start us, length us, event | category | flops | bytes accessed | tf_op | source)
XLA Modules:
  0.0 32.1 jit_solution(2732155202517764934)
XLA Ops:
  0.6 0.0 copy-start.1
  0.6 0.0 copy-start
  1.3 8.5 %shard_map.137 = (bf16[256,256]{1,0:T(8,128)(2,1)S(1)}, bf16[272,256]{1,0:T(8,128)(2,1)S(1)}) custom-call(s32[8,1,32]{2,1,0:T(1,128)} %own_ids.1, s32[8,10,1,32]{3,2,1,0:T(1,128)} %bitcast.6, s32[8,1,32]{2,1,0:T(1,128)} %hop_counts.1, s32[1,1,1,25]{3,2,1,0:T(1,128)} %bitcast.7, s32[1,1,1,112]{3,2,1,0:T(1,128)} %labels.1, bf16[2,128,256]{2,1,0:T(8,128)(2,1)} %weights.1, ...), custom_call_target="tpu_custom_call" | custom-call | tf_op jit(solution)/shard_map/pallas_call | solution.py:284
  9.8 5.1 %collective-permute-start = (bf16[272,256]{1,0:T(8,128)(2,1)S(1)}, bf16[272,256]{1,0:T(8,128)(2,1)S(1)}, u32[]{:S(2)}, u32[]{:S(2)}) collective-permute-start(bf16[272,256]{1,0:T(8,128)(2,1)S(1)} %get-tuple-element.22), channel_id=1, source_target_pairs={{0,12},{2,14},{4,8},{6,10},{8,4},{10,6},{12,0},{14,2},{1,13},{3,15... | collective-permute-start | bytes 417800 | tf_op jit(solution)/shard_map/ppermute | solution.py:329
  15.0 0.0 collective-permute-start.1
  15.0 1.3 %collective-permute-done.1.parts_b = bf16[256,256]{1,0:T(8,128)(2,1)S(1)} collective-permute-done((bf16[256,256]{1,0:T(8,128)(2,1)S(1)}, bf16[256,256]{1,0:T(8,128)(2,1)S(1)}, u32[]{:S(2)}, u32[]{:S(2)}) %collective-permute-start.1) | collective-permute-done | bytes 131104 | tf_op jit(solution)/shard_map/ppermute | solution.py:325
  16.3 2.4 %collective-permute-done = bf16[272,256]{1,0:T(8,128)(2,1)S(1)} collective-permute-done((bf16[272,256]{1,0:T(8,128)(2,1)S(1)}, bf16[272,256]{1,0:T(8,128)(2,1)S(1)}, u32[]{:S(2)}, u32[]{:S(2)}) %collective-permute-start) | collective-permute-done | bytes 139296 | tf_op jit(solution)/shard_map/ppermute | solution.py:329
  18.8 3.5 %collective-permute-start.4 = (bf16[272,256]{1,0:T(8,128)(2,1)S(1)}, bf16[272,256]{1,0:T(8,128)(2,1)S(1)}, u32[]{:S(2)}, u32[]{:S(2)}) collective-permute-start(bf16[272,256]{1,0:T(8,128)(2,1)S(1)} %add_convert_fusion.refs_0_), channel_id=1, source_target_pairs={{0,6},{2,4},{4,2},{6,0},{8,14},{10,12},{12,10},{14,8},{1,7},{3,5},... | collective-permute-start | bytes 417800 | tf_op jit(solution)/shard_map/ppermute | solution.py:329
  22.3 0.0 collective-permute-start.3
  22.3 0.6 %collective-permute-start.2 = (bf16[272,256]{1,0:T(8,128)(2,1)S(1)}, bf16[272,256]{1,0:T(8,128)(2,1)S(1)}, u32[]{:S(2)}, u32[]{:S(2)}) collective-permute-start(bf16[272,256]{1,0:T(8,128)(2,1)S(1)} %add_convert_fusion.refs_0_), channel_id=1, source_target_pairs={{0,2},{2,0},{4,6},{6,4},{8,10},{10,8},{12,14},{14,12},{1,3},{3,1},... | collective-permute-start | bytes 417800 | tf_op jit(solution)/shard_map/ppermute | solution.py:329
  23.0 3.8 %collective-permute-done.4.refs_3_ = bf16[272,256]{1,0:T(8,128)(2,1)S(1)} collective-permute-done((bf16[272,256]{1,0:T(8,128)(2,1)S(1)}, bf16[272,256]{1,0:T(8,128)(2,1)S(1)}, u32[]{:S(2)}, u32[]{:S(2)}) %collective-permute-start.4) | collective-permute-done | bytes 139296 | tf_op jit(solution)/shard_map/ppermute | solution.py:329
  26.8 1.0 %collective-permute-done.3.refs_2_ = bf16[272,256]{1,0:T(8,128)(2,1)S(1)} collective-permute-done((bf16[272,256]{1,0:T(8,128)(2,1)S(1)}, bf16[272,256]{1,0:T(8,128)(2,1)S(1)}, u32[]{:S(2)}, u32[]{:S(2)}) %collective-permute-start.3) | collective-permute-done | bytes 139296 | tf_op jit(solution)/shard_map/ppermute | solution.py:329
  27.8 0.5 %collective-permute-done.2.refs_1_ = bf16[272,256]{1,0:T(8,128)(2,1)S(1)} collective-permute-done((bf16[272,256]{1,0:T(8,128)(2,1)S(1)}, bf16[272,256]{1,0:T(8,128)(2,1)S(1)}, u32[]{:S(2)}, u32[]{:S(2)}) %collective-permute-start.2) | collective-permute-done | bytes 139296 | tf_op jit(solution)/shard_map/ppermute | solution.py:329
  28.3 0.0 copy-done.1
  28.3 0.0 copy-done
  28.3 1.3 %shard_map.138 = (bf16[32,256]{1,0:T(8,128)(2,1)}, f32[1,1]{1,0:T(1,128)}, bf16[304,256]{1,0:T(8,128)(2,1)S(1)}) custom-call(bf16[2,256,256]{2,1,0:T(8,128)(2,1)S(1)} %copy-done, bf16[112,256]{1,0:T(8,128)(2,1)S(1)} %bitcast.5, bf16[272,256]{1,0:T(8,128)(2,1)S(1)} %add_convert_fusion.refs_0_, bf16[272,256]{1,0:T(8,128)(2,1)S(1)} %collective-permute-done.2.refs_1_, ...), custom_call_target="tpu_custom_call" | custom-call | tf_op jit(solution)/shard_map/pallas_call | solution.py:333
  29.6 0.0 collective-permute-start.5
  29.6 0.3 %shard_map.139 = (f32[256,256]{1,0:T(8,128)S(1)}, f32[2,256,256]{2,1,0:T(8,128)S(1)}, f32[256,256]{1,0:T(8,128)S(1)}, bf16[256,256]{1,0:T(8,128)(2,1)S(1)}) custom-call(bf16[256,256]{1,0:T(8,128)(2,1)S(1)} %get-tuple-element.21.parts_a, bf16[304,256]{1,0:T(8,128)(2,1)S(1)} %get-tuple-element.26.pack_a, bf16[256,256]{1,0:T(8,128)(2,1)S(1)} %collective-permute-done.1.parts_b), custom_call_target="tpu_custom_call" | custom-call | tf_op jit(solution)/shard_map/pallas_call | solution.py:347
  30.0 1.1 %collective-permute-done.5.pack_b = bf16[304,256]{1,0:T(8,128)(2,1)S(1)} collective-permute-done((bf16[304,256]{1,0:T(8,128)(2,1)S(1)}, bf16[304,256]{1,0:T(8,128)(2,1)S(1)}, u32[]{:S(2)}, u32[]{:S(2)}) %collective-permute-start.5) | collective-permute-done | bytes 155680 | tf_op jit(solution)/shard_map/ppermute | solution.py:346
  31.0 1.1 %shard_map.140 = (f32[2,128,256]{2,1,0:T(8,128)}, f32[2,256,256]{2,1,0:T(8,128)}, f32[112,256]{1,0:T(8,128)}) custom-call(bf16[256,256]{1,0:T(8,128)(2,1)S(1)} %get-tuple-element.28.flipped, bf16[304,256]{1,0:T(8,128)(2,1)S(1)} %collective-permute-done.5.pack_b, f32[256,256]{1,0:T(8,128)S(1)} %get-tuple-element.29.one_a, ...), custom_call_target="tpu_custom_call" | custom-call | tf_op jit(solution)/shard_map/pallas_call | solution.py:359
  (1 shorter events, 0.0 us)
Async XLA Ops:
  0.6 27.6 %copy-start.1 = (bf16[256,112]{0,1:T(8,128)(2,1)S(1)}, bf16[256,112]{0,1:T(8,128)(2,1)}, u32[]{:S(2)}) copy-start(bf16[256,112]{0,1:T(8,128)(2,1)} %param.19) | copy-start | bytes 172036
  0.6 27.6 %copy-start = (bf16[2,256,256]{2,1,0:T(8,128)(2,1)S(1)}, bf16[2,256,256]{2,1,0:T(8,128)(2,1)}, u32[]{:S(2)}) copy-start(bf16[2,256,256]{2,1,0:T(8,128)(2,1)} %w_two.1) | copy-start | bytes 786436
  9.8 8.9 %collective-permute-start = (bf16[272,256]{1,0:T(8,128)(2,1)S(1)}, bf16[272,256]{1,0:T(8,128)(2,1)S(1)}, u32[]{:S(2)}, u32[]{:S(2)}) collective-permute-start(bf16[272,256]{1,0:T(8,128)(2,1)S(1)} %get-tuple-element.22), channel_id=1, source_target_pairs={{0,12},{2,14},{4,8},{6,10},{8,4},{10,6},{12,0},{14,2},{1,13},{3,15... | collective-permute-start | bytes 417800 | tf_op jit(solution)/shard_map/ppermute | solution.py:329
  15.0 1.3 %collective-permute-start.1 = (bf16[256,256]{1,0:T(8,128)(2,1)S(1)}, bf16[256,256]{1,0:T(8,128)(2,1)S(1)}, u32[]{:S(2)}, u32[]{:S(2)}) collective-permute-start(bf16[256,256]{1,0:T(8,128)(2,1)S(1)} %get-tuple-element.21.parts_a), channel_id=1, source_target_pairs={{0,1},{1,0},{2,3},{3,2},{4,5},{5,4},{6,7},{7,6},{8,9},{9,8},{10,11... | collective-permute-start | bytes 393224 | tf_op jit(solution)/shard_map/ppermute | solution.py:325
  18.8 8.0 %collective-permute-start.4 = (bf16[272,256]{1,0:T(8,128)(2,1)S(1)}, bf16[272,256]{1,0:T(8,128)(2,1)S(1)}, u32[]{:S(2)}, u32[]{:S(2)}) collective-permute-start(bf16[272,256]{1,0:T(8,128)(2,1)S(1)} %add_convert_fusion.refs_0_), channel_id=1, source_target_pairs={{0,6},{2,4},{4,2},{6,0},{8,14},{10,12},{12,10},{14,8},{1,7},{3,5},... | collective-permute-start | bytes 417800 | tf_op jit(solution)/shard_map/ppermute | solution.py:329
  22.3 5.5 %collective-permute-start.3 = (bf16[272,256]{1,0:T(8,128)(2,1)S(1)}, bf16[272,256]{1,0:T(8,128)(2,1)S(1)}, u32[]{:S(2)}, u32[]{:S(2)}) collective-permute-start(bf16[272,256]{1,0:T(8,128)(2,1)S(1)} %add_convert_fusion.refs_0_), channel_id=1, source_target_pairs={{0,4},{2,6},{4,0},{6,2},{8,12},{10,14},{12,8},{14,10},{1,5},{3,7},... | collective-permute-start | bytes 417800 | tf_op jit(solution)/shard_map/ppermute | solution.py:329
  22.3 6.0 %collective-permute-start.2 = (bf16[272,256]{1,0:T(8,128)(2,1)S(1)}, bf16[272,256]{1,0:T(8,128)(2,1)S(1)}, u32[]{:S(2)}, u32[]{:S(2)}) collective-permute-start(bf16[272,256]{1,0:T(8,128)(2,1)S(1)} %add_convert_fusion.refs_0_), channel_id=1, source_target_pairs={{0,2},{2,0},{4,6},{6,4},{8,10},{10,8},{12,14},{14,12},{1,3},{3,1},... | collective-permute-start | bytes 417800 | tf_op jit(solution)/shard_map/ppermute | solution.py:329
  29.6 1.4 %collective-permute-start.5 = (bf16[304,256]{1,0:T(8,128)(2,1)S(1)}, bf16[304,256]{1,0:T(8,128)(2,1)S(1)}, u32[]{:S(2)}, u32[]{:S(2)}) collective-permute-start(bf16[304,256]{1,0:T(8,128)(2,1)S(1)} %get-tuple-element.26.pack_a), channel_id=1, source_target_pairs={{0,1},{1,0},{2,3},{3,2},{4,5},{5,4},{6,7},{7,6},{8,9},{9,8},{10,11... | collective-permute-start | bytes 466952 | tf_op jit(solution)/shard_map/ppermute | solution.py:346

commit v5 on v4

--- a/solution.py
+++ b/solution.py
@@ -197,7 +197,7 @@
     soft = jnp.maximum(logits, 0.0) + jnp.log1p(jnp.exp(-jnp.abs(logits)))
     losses = jnp.mean(soft - target * logits, axis=1, keepdims=True)
     chosen = lax.broadcasted_iota(jnp.int32, losses.shape, 0) == me
-    loss_ref[...] = jnp.sum(jnp.where(chosen, losses, 0.0), axis=0, keepdims=True)
+    loss_ref[...] = jnp.broadcast_to(jnp.sum(jnp.where(chosen, losses, 0.0), axis=0, keepdims=True), loss_ref.shape)
     grad_logits = (jax.nn.sigmoid(logits) - target).astype(BF)
     back_two = dot(grad_logits, w_three[...])
     grad_two = (back_two * silu_slope(pre_two, sig_two)).astype(BF)
@@ -236,7 +236,11 @@
     return one, dot(part(0), part(2), TN), dot(part(1), part(2), TN), dot(part(4), part(3), TN)
 
 
-def half_kernel(batches, parts_a, pack_a, parts_b, one_ref, two_ref, three_ref, flipped_ref):
+def half_kernel(
+    batches, parts_a, pack_a, parts_b, hidden, loss, one_ref, two_ref, three_ref, flipped_ref, hidden_ref, loss_ref
+):
+    hidden_ref[...] = hidden[...]
+    loss_ref[...] = loss[:1, :1]
     one, seeds, means, three = products(batches, parts_a[...].T, pack_a)
     one_ref[...] = one
     two_ref[0] = seeds
@@ -275,7 +279,7 @@
     fan = hop_two.shape[2]
     label_count = weight_three.shape[1]
     rows = groups * block_rows
-    meta_rows = -(-groups // 16) * 16
+    meta_rows = -(-groups // 8) * 8
     labels_at = width // 2
     chunks = 16
     mib = 2**20
@@ -334,7 +338,7 @@
         functools.partial(upper_kernel, groups, block_rows, labels_at),
         out_shape=(
             jax.ShapeDtypeStruct((block_rows, width), BF),
-            jax.ShapeDtypeStruct((1, 1), F32),
+            jax.ShapeDtypeStruct((8, 128), F32),
             jax.ShapeDtypeStruct((rows + 6 * groups, width), BF),
         ),
         in_specs=[VMEM] * (len(terms) + 2),
@@ -344,18 +348,20 @@
     )(weight_two, weight_three.T, *terms)
 
     pack_b = lax.ppermute(pack, "sub", swap)
-    one, two, three, flipped_b = pl.pallas_call(
+    one, two, three, flipped_b, hidden, loss = pl.pallas_call(
         functools.partial(half_kernel, groups),
         out_shape=(
             jax.ShapeDtypeStruct((2 * depth, width), F32),
             jax.ShapeDtypeStruct((2, width, width), F32),
             jax.ShapeDtypeStruct((width, width), F32),
             jax.ShapeDtypeStruct((2 * depth, rows), BF),
-        ),
-        in_specs=[VMEM] * 3,
-        out_specs=(VMEM,) * 4,
+            jax.ShapeDtypeStruct((block_rows, width), BF),
+            jax.ShapeDtypeStruct((1, 1), F32),
+        ),
+        in_specs=[VMEM] * 5,
+        out_specs=(VMEM,) * 6,
         compiler_params=pltpu.CompilerParams(vmem_limit_bytes=6 * mib + 4 * row_bytes),
-    )(parts, pack, parts_b)
+    )(parts, pack, parts_b, hidden, loss)
     grad_one, grad_two, grad_three = pl.pallas_call(
         functools.partial(final_kernel, groups),
         out_shape=(

time: 32.3 us -> 31.6 us (0.978)
  waiting for transfers between devices: 10.1 us -> 9.33 us
    ppermute x1, waiting for transfers between devices: 1.05 us -> 0.51 us  [per_device(): pack_b = lax.ppermute(pack, 'sub', swap)]
    pallas_call x1, Pallas kernels: 0.32 us -> 0.85 us  [per_device(): pl.pallas_call(functools.partial(half_kernel, groups), out_shape=(jax.Sha...]
    pallas_call x1, Pallas kernels: 1.34 us -> 0.91 us  [per_device(): pl.pallas_call(functools.partial(upper_kernel, groups, block_rows, labels...]
  transfers between devices with their start and end apart: 6 -> 6, of which waited for: 6 -> 6; matrix products, arithmetic and copies ran while one was open for 0% -> 0% of each run, Pallas kernels for 1% -> 3%
where the time goes in v5:
time: 31.6 us; the launch traced here: 31.4 us
  Pallas kernels  11.4 us (36%)
  waiting for transfers between devices  9.33 us (30%)
  starting transfers between devices  9.31 us (29%)
  between operations  1.37 us (4%)
    ppermute x4, starting transfers between devices, per_device(): lax.ppermute(pre, 'col', [(i, i ^ m) for i in range(groups)])  9.24 us
    pallas_call x1, Pallas kernels, per_device(): pl.pallas_call(functools.partial(gather_kernel, chunks, 256, 16, labels_a...  8.49 us
    ppermute x4, waiting for transfers between devices, per_device(): lax.ppermute(pre, 'col', [(i, i ^ m) for i in range(groups)])  7.47 us
    ppermute x1, waiting for transfers between devices, per_device(): parts_b = lax.ppermute(parts, 'sub', swap)  1.35 us
    pallas_call x1, Pallas kernels, per_device(): pl.pallas_call(functools.partial(final_kernel, groups), out_shape=(jax.Sh...  1.13 us
    pallas_call x1, Pallas kernels, per_device(): pl.pallas_call(functools.partial(upper_kernel, groups, block_rows, labels...  0.91 us
    pallas_call x1, Pallas kernels, per_device(): pl.pallas_call(functools.partial(half_kernel, groups), out_shape=(jax.Sha...  0.85 us
  transfers between devices with their start and end apart: 6, of which 6 were waited for; matrix products, arithmetic and copies ran while one was open for 0% of the time, Pallas kernels for 3%

profile of v5, /device:TPU:0, one launch (start us, length us, event | category | flops | bytes accessed | tf_op | source)
XLA Modules:
  0.0 31.4 jit_solution(1877253781135621868)
XLA Ops:
  0.6 0.0 copy-start.1
  0.6 0.0 copy-start
  1.3 8.5 %shard_map.137 = (bf16[256,256]{1,0:T(8,128)(2,1)S(1)}, bf16[264,256]{1,0:T(8,128)(2,1)S(1)}) custom-call(s32[8,1,32]{2,1,0:T(1,128)} %own_ids.1, s32[8,10,1,32]{3,2,1,0:T(1,128)} %bitcast.6, s32[8,1,32]{2,1,0:T(1,128)} %hop_counts.1, s32[1,1,1,25]{3,2,1,0:T(1,128)} %bitcast.7, s32[1,1,1,112]{3,2,1,0:T(1,128)} %labels.1, bf16[2,128,256]{2,1,0:T(8,128)(2,1)} %weights.1, ...), custom_call_target="tpu_custom_call" | custom-call | tf_op jit(solution)/shard_map/pallas_call | solution.py:288
  9.8 5.1 %collective-permute-start = (bf16[264,256]{1,0:T(8,128)(2,1)S(1)}, bf16[264,256]{1,0:T(8,128)(2,1)S(1)}, u32[]{:S(2)}, u32[]{:S(2)}) collective-permute-start(bf16[264,256]{1,0:T(8,128)(2,1)S(1)} %get-tuple-element.24), channel_id=1, source_target_pairs={{0,12},{2,14},{4,8},{6,10},{8,4},{10,6},{12,0},{14,2},{1,13},{3,15... | collective-permute-start | bytes 405512 | tf_op jit(solution)/shard_map/ppermute | solution.py:333
  15.0 0.0 collective-permute-start.1
  15.0 1.3 %collective-permute-done.1.parts_b = bf16[256,256]{1,0:T(8,128)(2,1)S(1)} collective-permute-done((bf16[256,256]{1,0:T(8,128)(2,1)S(1)}, bf16[256,256]{1,0:T(8,128)(2,1)S(1)}, u32[]{:S(2)}, u32[]{:S(2)}) %collective-permute-start.1) | collective-permute-done | bytes 131104 | tf_op jit(solution)/shard_map/ppermute | solution.py:329
  16.3 2.3 %collective-permute-done = bf16[264,256]{1,0:T(8,128)(2,1)S(1)} collective-permute-done((bf16[264,256]{1,0:T(8,128)(2,1)S(1)}, bf16[264,256]{1,0:T(8,128)(2,1)S(1)}, u32[]{:S(2)}, u32[]{:S(2)}) %collective-permute-start) | collective-permute-done | bytes 135200 | tf_op jit(solution)/shard_map/ppermute | solution.py:333
  18.7 3.5 %collective-permute-start.4 = (bf16[264,256]{1,0:T(8,128)(2,1)S(1)}, bf16[264,256]{1,0:T(8,128)(2,1)S(1)}, u32[]{:S(2)}, u32[]{:S(2)}) collective-permute-start(bf16[264,256]{1,0:T(8,128)(2,1)S(1)} %add_convert_fusion.refs_0_), channel_id=1, source_target_pairs={{0,6},{2,4},{4,2},{6,0},{8,14},{10,12},{12,10},{14,8},{1,7},{3,5},... | collective-permute-start | bytes 405512 | tf_op jit(solution)/shard_map/ppermute | solution.py:333
  22.1 0.0 collective-permute-start.3
  22.1 0.6 %collective-permute-start.2 = (bf16[264,256]{1,0:T(8,128)(2,1)S(1)}, bf16[264,256]{1,0:T(8,128)(2,1)S(1)}, u32[]{:S(2)}, u32[]{:S(2)}) collective-permute-start(bf16[264,256]{1,0:T(8,128)(2,1)S(1)} %add_convert_fusion.refs_0_), channel_id=1, source_target_pairs={{0,2},{2,0},{4,6},{6,4},{8,10},{10,8},{12,14},{14,12},{1,3},{3,1},... | collective-permute-start | bytes 405512 | tf_op jit(solution)/shard_map/ppermute | solution.py:333
  22.8 3.8 %collective-permute-done.4.refs_3_ = bf16[264,256]{1,0:T(8,128)(2,1)S(1)} collective-permute-done((bf16[264,256]{1,0:T(8,128)(2,1)S(1)}, bf16[264,256]{1,0:T(8,128)(2,1)S(1)}, u32[]{:S(2)}, u32[]{:S(2)}) %collective-permute-start.4) | collective-permute-done | bytes 135200 | tf_op jit(solution)/shard_map/ppermute | solution.py:333
  26.6 1.0 %collective-permute-done.3.refs_2_ = bf16[264,256]{1,0:T(8,128)(2,1)S(1)} collective-permute-done((bf16[264,256]{1,0:T(8,128)(2,1)S(1)}, bf16[264,256]{1,0:T(8,128)(2,1)S(1)}, u32[]{:S(2)}, u32[]{:S(2)}) %collective-permute-start.3) | collective-permute-done | bytes 135200 | tf_op jit(solution)/shard_map/ppermute | solution.py:333
  27.5 0.4 %collective-permute-done.2.refs_1_ = bf16[264,256]{1,0:T(8,128)(2,1)S(1)} collective-permute-done((bf16[264,256]{1,0:T(8,128)(2,1)S(1)}, bf16[264,256]{1,0:T(8,128)(2,1)S(1)}, u32[]{:S(2)}, u32[]{:S(2)}) %collective-permute-start.2) | collective-permute-done | bytes 135200 | tf_op jit(solution)/shard_map/ppermute | solution.py:333
  27.9 0.0 copy-done.1
  27.9 0.0 copy-done
  27.9 0.9 %shard_map.138 = (bf16[32,256]{1,0:T(8,128)(2,1)S(1)}, f32[8,128]{1,0:T(8,128)S(1)}, bf16[304,256]{1,0:T(8,128)(2,1)S(1)}) custom-call(bf16[2,256,256]{2,1,0:T(8,128)(2,1)S(1)} %copy-done, bf16[112,256]{1,0:T(8,128)(2,1)S(1)} %bitcast.5, bf16[264,256]{1,0:T(8,128)(2,1)S(1)} %add_convert_fusion.refs_0_, bf16[264,256]{1,0:T(8,128)(2,1)S(1)} %collective-permute-done.2.refs_1_, ...), custom_call_target="tpu_custom_call" | custom-call | tf_op jit(solution)/shard_map/pallas_call | solution.py:337
  28.9 0.1 collective-permute-start.5
  28.9 0.9 %shard_map.139 = (f32[256,256]{1,0:T(8,128)S(1)}, f32[2,256,256]{2,1,0:T(8,128)S(1)}, f32[256,256]{1,0:T(8,128)S(1)}, bf16[256,256]{1,0:T(8,128)(2,1)S(1)}, bf16[32,256]{1,0:T(8,128)(2,1)}, /*index=5*/f32[1,1]{1,0:T(1,128)}) custom-call(bf16[256,256]{1,0:T(8,128)(2,1)S(1)} %get-tuple-element.22.parts_a, bf16[304,256]{1,0:T(8,128)(2,1)S(1)} %get-tuple-element.26.pack_a, ...), custom_call_target="tpu_custom_call" | custom-call | tf_op jit(solution)/shard_map/pallas_call | solution.py:351
  29.8 0.5 %collective-permute-done.5.pack_b = bf16[304,256]{1,0:T(8,128)(2,1)S(1)} collective-permute-done((bf16[304,256]{1,0:T(8,128)(2,1)S(1)}, bf16[304,256]{1,0:T(8,128)(2,1)S(1)}, u32[]{:S(2)}, u32[]{:S(2)}) %collective-permute-start.5) | collective-permute-done | bytes 155680 | tf_op jit(solution)/shard_map/ppermute | solution.py:350
  30.3 1.1 %shard_map.140 = (f32[2,128,256]{2,1,0:T(8,128)}, f32[2,256,256]{2,1,0:T(8,128)}, f32[112,256]{1,0:T(8,128)}) custom-call(bf16[256,256]{1,0:T(8,128)(2,1)S(1)} %get-tuple-element.32.flipped, bf16[304,256]{1,0:T(8,128)(2,1)S(1)} %collective-permute-done.5.pack_b, f32[256,256]{1,0:T(8,128)S(1)} %get-tuple-element.33.one_a, ...), custom_call_target="tpu_custom_call" | custom-call | tf_op jit(solution)/shard_map/pallas_call | solution.py:365
  (1 shorter events, 0.0 us)
Async XLA Ops:
  0.6 27.3 %copy-start.1 = (bf16[256,112]{0,1:T(8,128)(2,1)S(1)}, bf16[256,112]{0,1:T(8,128)(2,1)}, u32[]{:S(2)}) copy-start(bf16[256,112]{0,1:T(8,128)(2,1)} %param.19) | copy-start | bytes 172036
  0.6 27.3 %copy-start = (bf16[2,256,256]{2,1,0:T(8,128)(2,1)S(1)}, bf16[2,256,256]{2,1,0:T(8,128)(2,1)}, u32[]{:S(2)}) copy-start(bf16[2,256,256]{2,1,0:T(8,128)(2,1)} %w_two.1) | copy-start | bytes 786436
  9.8 8.8 %collective-permute-start = (bf16[264,256]{1,0:T(8,128)(2,1)S(1)}, bf16[264,256]{1,0:T(8,128)(2,1)S(1)}, u32[]{:S(2)}, u32[]{:S(2)}) collective-permute-start(bf16[264,256]{1,0:T(8,128)(2,1)S(1)} %get-tuple-element.24), channel_id=1, source_target_pairs={{0,12},{2,14},{4,8},{6,10},{8,4},{10,6},{12,0},{14,2},{1,13},{3,15... | collective-permute-start | bytes 405512 | tf_op jit(solution)/shard_map/ppermute | solution.py:333
  15.0 1.3 %collective-permute-start.1 = (bf16[256,256]{1,0:T(8,128)(2,1)S(1)}, bf16[256,256]{1,0:T(8,128)(2,1)S(1)}, u32[]{:S(2)}, u32[]{:S(2)}) collective-permute-start(bf16[256,256]{1,0:T(8,128)(2,1)S(1)} %get-tuple-element.22.parts_a), channel_id=1, source_target_pairs={{0,1},{1,0},{2,3},{3,2},{4,5},{5,4},{6,7},{7,6},{8,9},{9,8},{10,11... | collective-permute-start | bytes 393224 | tf_op jit(solution)/shard_map/ppermute | solution.py:329
  18.7 7.9 %collective-permute-start.4 = (bf16[264,256]{1,0:T(8,128)(2,1)S(1)}, bf16[264,256]{1,0:T(8,128)(2,1)S(1)}, u32[]{:S(2)}, u32[]{:S(2)}) collective-permute-start(bf16[264,256]{1,0:T(8,128)(2,1)S(1)} %add_convert_fusion.refs_0_), channel_id=1, source_target_pairs={{0,6},{2,4},{4,2},{6,0},{8,14},{10,12},{12,10},{14,8},{1,7},{3,5},... | collective-permute-start | bytes 405512 | tf_op jit(solution)/shard_map/ppermute | solution.py:333
  22.1 5.4 %collective-permute-start.3 = (bf16[264,256]{1,0:T(8,128)(2,1)S(1)}, bf16[264,256]{1,0:T(8,128)(2,1)S(1)}, u32[]{:S(2)}, u32[]{:S(2)}) collective-permute-start(bf16[264,256]{1,0:T(8,128)(2,1)S(1)} %add_convert_fusion.refs_0_), channel_id=1, source_target_pairs={{0,4},{2,6},{4,0},{6,2},{8,12},{10,14},{12,8},{14,10},{1,5},{3,7},... | collective-permute-start | bytes 405512 | tf_op jit(solution)/shard_map/ppermute | solution.py:333
  22.1 5.8 %collective-permute-start.2 = (bf16[264,256]{1,0:T(8,128)(2,1)S(1)}, bf16[264,256]{1,0:T(8,128)(2,1)S(1)}, u32[]{:S(2)}, u32[]{:S(2)}) collective-permute-start(bf16[264,256]{1,0:T(8,128)(2,1)S(1)} %add_convert_fusion.refs_0_), channel_id=1, source_target_pairs={{0,2},{2,0},{4,6},{6,4},{8,10},{10,8},{12,14},{14,12},{1,3},{3,1},... | collective-permute-start | bytes 405512 | tf_op jit(solution)/shard_map/ppermute | solution.py:333
  28.9 1.4 %collective-permute-start.5 = (bf16[304,256]{1,0:T(8,128)(2,1)S(1)}, bf16[304,256]{1,0:T(8,128)(2,1)S(1)}, u32[]{:S(2)}, u32[]{:S(2)}) collective-permute-start(bf16[304,256]{1,0:T(8,128)(2,1)S(1)} %get-tuple-element.26.pack_a), channel_id=1, source_target_pairs={{0,1},{1,0},{2,3},{3,2},{4,5},{5,4},{6,7},{7,6},{8,9},{9,8},{10,11... | collective-permute-start | bytes 466952 | tf_op jit(solution)/shard_map/ppermute | solution.py:350

commit v6 on v5

--- a/solution.py
+++ b/solution.py
@@ -30,13 +30,10 @@
 
 def phases(groups):
     bits = groups.bit_length() - 1
-    plan = []
+    plan = [[1 << k, 2 << k, 3 << k] for k in range(0, bits - 1, 2)]
     if bits % 2:
-        bits -= 1
-        plan.append([(1 << bits) | (1 << bits >> 1)])
-    while bits:
-        bits -= 2
-        plan.append([1 << bits, 2 << bits, 3 << bits])
+        top = 1 << (bits - 1)
+        plan.append([top | top >> 1])
     return plan
 
 
@@ -120,7 +117,7 @@
                 at = pl.multiple_of((i * unroll + u) * block, block)
                 part = stage[k, :, pl.ds(at, block)]
                 if depth % 128 == 0:
-                    flipped = part.T.astype(F32) if u % 4 else dot(eye, part, NT)
+                    flipped = part.T.astype(F32) if u % 4 != 1 else dot(eye, part, NT)
                 else:
                     flipped = part.astype(F32).T
                 rows_f32[pl.ds(pl.multiple_of(k * span + at, block), block), :] = flipped
@@ -169,7 +166,7 @@
     batches, block_rows, labels_at, w_two, w_three, *refs
 ):
     *terms, hidden_ref, loss_ref, pack_ref, hidden_f32 = refs
-    rows, width = pack_ref.shape[0] - 6 * batches, pack_ref.shape[1]
+    rows, width = pack_ref.shape[0] - 5 * batches, pack_ref.shape[1]
     me = lax.axis_index("col")
     label_count = w_three.shape[0]
     pre_one = add_up([term[:rows, :] for term in terms])
@@ -217,7 +214,6 @@
             grad_two.astype(F32),
             hidden_two.astype(F32),
             jnp.concatenate([grad_logits.astype(F32), blank], axis=1),
-            jnp.zeros((batches, width), F32),
         ],
         axis=0,
     )
@@ -339,7 +335,7 @@
         out_shape=(
             jax.ShapeDtypeStruct((block_rows, width), BF),
             jax.ShapeDtypeStruct((8, 128), F32),
-            jax.ShapeDtypeStruct((rows + 6 * groups, width), BF),
+            jax.ShapeDtypeStruct((rows + 5 * groups, width), BF),
         ),
         in_specs=[VMEM] * (len(terms) + 2),
         out_specs=(VMEM, VMEM, VMEM),

time: 31.6 us -> 31.4 us (level)
  starting transfers between devices: 9.31 us -> 8.35 us
  waiting for transfers between devices: 9.33 us -> 9.84 us
    ppermute x4, starting transfers between devices: 9.24 us -> 8.28 us  [per_device(): lax.ppermute(pre, 'col', [(i, i ^ m) for i in range(groups)])]
    ppermute x4, waiting for transfers between devices: 7.47 us -> 7.99 us  [per_device(): lax.ppermute(pre, 'col', [(i, i ^ m) for i in range(groups)])]
  transfers between devices with their start and end apart: 6 -> 6, of which waited for: 6 -> 5; matrix products, arithmetic and copies ran while one was open for 0% -> 0% of each run, Pallas kernels for 3% -> 3%
where the time goes in v6:
time: 31.4 us; the launch traced here: 31 us
  Pallas kernels  11.3 us (36%)
  waiting for transfers between devices  9.84 us (31%)
  starting transfers between devices  8.35 us (27%)
  between operations  1.37 us (4%)
    pallas_call x1, Pallas kernels, per_device(): pl.pallas_call(functools.partial(gather_kernel, chunks, 256, 16, labels_a...  8.48 us
    ppermute x4, starting transfers between devices, per_device(): lax.ppermute(pre, 'col', [(i, i ^ m) for i in range(groups)])  8.28 us
    ppermute x4, waiting for transfers between devices, per_device(): lax.ppermute(pre, 'col', [(i, i ^ m) for i in range(groups)])  7.99 us
    ppermute x1, waiting for transfers between devices, per_device(): parts_b = lax.ppermute(parts, 'sub', swap)  1.35 us
    pallas_call x1, Pallas kernels, per_device(): pl.pallas_call(functools.partial(final_kernel, groups), out_shape=(jax.Sh...  1.13 us
    pallas_call x1, Pallas kernels, per_device(): pl.pallas_call(functools.partial(upper_kernel, groups, block_rows, labels...  0.86 us
    pallas_call x1, Pallas kernels, per_device(): pl.pallas_call(functools.partial(half_kernel, groups), out_shape=(jax.Sha...  0.85 us
  transfers between devices with their start and end apart: 6, of which 5 were waited for; matrix products, arithmetic and copies ran while one was open for 0% of the time, Pallas kernels for 3%

profile of v6, /device:TPU:0, one launch (start us, length us, event | category | flops | bytes accessed | tf_op | source)
XLA Modules:
  0.0 31.0 jit_solution(200532078091882468)
XLA Ops:
  0.6 0.0 copy-start.1
  0.6 0.0 copy-start
  1.3 8.5 %shard_map.137 = (bf16[256,256]{1,0:T(8,128)(2,1)S(1)}, bf16[264,256]{1,0:T(8,128)(2,1)S(1)}) custom-call(s32[8,1,32]{2,1,0:T(1,128)} %own_ids.1, s32[8,10,1,32]{3,2,1,0:T(1,128)} %bitcast.6, s32[8,1,32]{2,1,0:T(1,128)} %hop_counts.1, s32[1,1,1,25]{3,2,1,0:T(1,128)} %bitcast.7, s32[1,1,1,112]{3,2,1,0:T(1,128)} %labels.1, bf16[2,128,256]{2,1,0:T(8,128)(2,1)} %weights.1, ...), custom_call_target="tpu_custom_call" | custom-call | tf_op jit(solution)/shard_map/pallas_call | solution.py:284
  9.8 4.0 %collective-permute-start.2 = (bf16[264,256]{1,0:T(8,128)(2,1)S(1)}, bf16[264,256]{1,0:T(8,128)(2,1)S(1)}, u32[]{:S(2)}, u32[]{:S(2)}) collective-permute-start(bf16[264,256]{1,0:T(8,128)(2,1)S(1)} %get-tuple-element.26), channel_id=1, source_target_pairs={{0,6},{2,4},{4,2},{6,0},{8,14},{10,12},{12,10},{14,8},{1,7},{3,5},... | collective-permute-start | bytes 405512 | tf_op jit(solution)/shard_map/ppermute | solution.py:329
  13.9 0.4 %collective-permute-start.1 = (bf16[264,256]{1,0:T(8,128)(2,1)S(1)}, bf16[264,256]{1,0:T(8,128)(2,1)S(1)}, u32[]{:S(2)}, u32[]{:S(2)}) collective-permute-start(bf16[264,256]{1,0:T(8,128)(2,1)S(1)} %get-tuple-element.26), channel_id=1, source_target_pairs={{0,4},{2,6},{4,0},{6,2},{8,12},{10,14},{12,8},{14,10},{1,5},{3,7},... | collective-permute-start | bytes 405512 | tf_op jit(solution)/shard_map/ppermute | solution.py:329
  14.3 0.2 collective-permute-start
  14.5 0.0 collective-permute-start.3
  14.5 1.3 %collective-permute-done.3.parts_b = bf16[256,256]{1,0:T(8,128)(2,1)S(1)} collective-permute-done((bf16[256,256]{1,0:T(8,128)(2,1)S(1)}, bf16[256,256]{1,0:T(8,128)(2,1)S(1)}, u32[]{:S(2)}, u32[]{:S(2)}) %collective-permute-start.3) | collective-permute-done | bytes 131104 | tf_op jit(solution)/shard_map/ppermute | solution.py:325
  15.8 2.4 %collective-permute-done.2 = bf16[264,256]{1,0:T(8,128)(2,1)S(1)} collective-permute-done((bf16[264,256]{1,0:T(8,128)(2,1)S(1)}, bf16[264,256]{1,0:T(8,128)(2,1)S(1)}, u32[]{:S(2)}, u32[]{:S(2)}) %collective-permute-start.2) | collective-permute-done | bytes 135200 | tf_op jit(solution)/shard_map/ppermute | solution.py:329
  18.3 2.2 %collective-permute-done.1 = bf16[264,256]{1,0:T(8,128)(2,1)S(1)} collective-permute-done((bf16[264,256]{1,0:T(8,128)(2,1)S(1)}, bf16[264,256]{1,0:T(8,128)(2,1)S(1)}, u32[]{:S(2)}, u32[]{:S(2)}) %collective-permute-start.1) | collective-permute-done | bytes 135200 | tf_op jit(solution)/shard_map/ppermute | solution.py:329
  20.5 0.0 collective-permute-done
  20.5 0.1 add_convert_fusion.refs_0_
  20.6 3.6 %collective-permute-start.4 = (bf16[264,256]{1,0:T(8,128)(2,1)S(1)}, bf16[264,256]{1,0:T(8,128)(2,1)S(1)}, u32[]{:S(2)}, u32[]{:S(2)}) collective-permute-start(bf16[264,256]{1,0:T(8,128)(2,1)S(1)} %add_convert_fusion.refs_0_), channel_id=1, source_target_pairs={{0,12},{2,14},{4,8},{6,10},{8,4},{10,6},{12,0},{14,2},{1,13},{3,15... | collective-permute-start | bytes 405512 | tf_op jit(solution)/shard_map/ppermute | solution.py:329
  24.2 3.3 %collective-permute-done.4.refs_1_ = bf16[264,256]{1,0:T(8,128)(2,1)S(1)} collective-permute-done((bf16[264,256]{1,0:T(8,128)(2,1)S(1)}, bf16[264,256]{1,0:T(8,128)(2,1)S(1)}, u32[]{:S(2)}, u32[]{:S(2)}) %collective-permute-start.4) | collective-permute-done | bytes 135200 | tf_op jit(solution)/shard_map/ppermute | solution.py:329
  27.5 0.0 copy-done.1
  27.5 0.0 copy-done
  27.5 0.9 %shard_map.138 = (bf16[32,256]{1,0:T(8,128)(2,1)S(1)}, f32[8,128]{1,0:T(8,128)S(1)}, bf16[296,256]{1,0:T(8,128)(2,1)S(1)}) custom-call(bf16[2,256,256]{2,1,0:T(8,128)(2,1)S(1)} %copy-done, bf16[112,256]{1,0:T(8,128)(2,1)S(1)} %bitcast.5, bf16[264,256]{1,0:T(8,128)(2,1)S(1)} %add_convert_fusion.refs_0_, bf16[264,256]{1,0:T(8,128)(2,1)S(1)} %collective-permute-done.4.refs_1_), custom_call_target="tpu_custom_call" | custom-call | tf_op jit(solution)/shard_map/pallas_call | solution.py:333
  28.4 0.1 collective-permute-start.5
  28.5 0.9 %shard_map.139 = (f32[256,256]{1,0:T(8,128)S(1)}, f32[2,256,256]{2,1,0:T(8,128)S(1)}, f32[256,256]{1,0:T(8,128)S(1)}, bf16[256,256]{1,0:T(8,128)(2,1)S(1)}, bf16[32,256]{1,0:T(8,128)(2,1)}, /*index=5*/f32[1,1]{1,0:T(1,128)}) custom-call(bf16[256,256]{1,0:T(8,128)(2,1)S(1)} %get-tuple-element.24.parts_a, bf16[296,256]{1,0:T(8,128)(2,1)S(1)} %get-tuple-element.30.pack_a, ...), custom_call_target="tpu_custom_call" | custom-call | tf_op jit(solution)/shard_map/pallas_call | solution.py:347
  29.3 0.5 %collective-permute-done.5.pack_b = bf16[296,256]{1,0:T(8,128)(2,1)S(1)} collective-permute-done((bf16[296,256]{1,0:T(8,128)(2,1)S(1)}, bf16[296,256]{1,0:T(8,128)(2,1)S(1)}, u32[]{:S(2)}, u32[]{:S(2)}) %collective-permute-start.5) | collective-permute-done | bytes 151584 | tf_op jit(solution)/shard_map/ppermute | solution.py:346
  29.8 1.1 %shard_map.140 = (f32[2,128,256]{2,1,0:T(8,128)}, f32[2,256,256]{2,1,0:T(8,128)}, f32[112,256]{1,0:T(8,128)}) custom-call(bf16[256,256]{1,0:T(8,128)(2,1)S(1)} %get-tuple-element.36.flipped, bf16[296,256]{1,0:T(8,128)(2,1)S(1)} %collective-permute-done.5.pack_b, f32[256,256]{1,0:T(8,128)S(1)} %get-tuple-element.37.one_a, ...), custom_call_target="tpu_custom_call" | custom-call | tf_op jit(solution)/shard_map/pallas_call | solution.py:361
Async XLA Ops:
  0.6 26.9 %copy-start.1 = (bf16[256,112]{0,1:T(8,128)(2,1)S(1)}, bf16[256,112]{0,1:T(8,128)(2,1)}, u32[]{:S(2)}) copy-start(bf16[256,112]{0,1:T(8,128)(2,1)} %param.19) | copy-start | bytes 172036
  0.6 26.9 %copy-start = (bf16[2,256,256]{2,1,0:T(8,128)(2,1)S(1)}, bf16[2,256,256]{2,1,0:T(8,128)(2,1)}, u32[]{:S(2)}) copy-start(bf16[2,256,256]{2,1,0:T(8,128)(2,1)} %w_two.1) | copy-start | bytes 786436
  9.8 8.4 %collective-permute-start.2 = (bf16[264,256]{1,0:T(8,128)(2,1)S(1)}, bf16[264,256]{1,0:T(8,128)(2,1)S(1)}, u32[]{:S(2)}, u32[]{:S(2)}) collective-permute-start(bf16[264,256]{1,0:T(8,128)(2,1)S(1)} %get-tuple-element.26), channel_id=1, source_target_pairs={{0,6},{2,4},{4,2},{6,0},{8,14},{10,12},{12,10},{14,8},{1,7},{3,5},... | collective-permute-start | bytes 405512 | tf_op jit(solution)/shard_map/ppermute | solution.py:329
  13.9 6.7 %collective-permute-start.1 = (bf16[264,256]{1,0:T(8,128)(2,1)S(1)}, bf16[264,256]{1,0:T(8,128)(2,1)S(1)}, u32[]{:S(2)}, u32[]{:S(2)}) collective-permute-start(bf16[264,256]{1,0:T(8,128)(2,1)S(1)} %get-tuple-element.26), channel_id=1, source_target_pairs={{0,4},{2,6},{4,0},{6,2},{8,12},{10,14},{12,8},{14,10},{1,5},{3,7},... | collective-permute-start | bytes 405512 | tf_op jit(solution)/shard_map/ppermute | solution.py:329
  14.3 6.3 %collective-permute-start = (bf16[264,256]{1,0:T(8,128)(2,1)S(1)}, bf16[264,256]{1,0:T(8,128)(2,1)S(1)}, u32[]{:S(2)}, u32[]{:S(2)}) collective-permute-start(bf16[264,256]{1,0:T(8,128)(2,1)S(1)} %get-tuple-element.26), channel_id=1, source_target_pairs={{0,2},{2,0},{4,6},{6,4},{8,10},{10,8},{12,14},{14,12},{1,3},{3,1},... | collective-permute-start | bytes 405512 | tf_op jit(solution)/shard_map/ppermute | solution.py:329
  14.5 1.3 %collective-permute-start.3 = (bf16[256,256]{1,0:T(8,128)(2,1)S(1)}, bf16[256,256]{1,0:T(8,128)(2,1)S(1)}, u32[]{:S(2)}, u32[]{:S(2)}) collective-permute-start(bf16[256,256]{1,0:T(8,128)(2,1)S(1)} %get-tuple-element.24.parts_a), channel_id=1, source_target_pairs={{0,1},{1,0},{2,3},{3,2},{4,5},{5,4},{6,7},{7,6},{8,9},{9,8},{10,11... | collective-permute-start | bytes 393224 | tf_op jit(solution)/shard_map/ppermute | solution.py:325
  20.6 6.9 %collective-permute-start.4 = (bf16[264,256]{1,0:T(8,128)(2,1)S(1)}, bf16[264,256]{1,0:T(8,128)(2,1)S(1)}, u32[]{:S(2)}, u32[]{:S(2)}) collective-permute-start(bf16[264,256]{1,0:T(8,128)(2,1)S(1)} %add_convert_fusion.refs_0_), channel_id=1, source_target_pairs={{0,12},{2,14},{4,8},{6,10},{8,4},{10,6},{12,0},{14,2},{1,13},{3,15... | collective-permute-start | bytes 405512 | tf_op jit(solution)/shard_map/ppermute | solution.py:329
  28.4 1.4 %collective-permute-start.5 = (bf16[296,256]{1,0:T(8,128)(2,1)S(1)}, bf16[296,256]{1,0:T(8,128)(2,1)S(1)}, u32[]{:S(2)}, u32[]{:S(2)}) collective-permute-start(bf16[296,256]{1,0:T(8,128)(2,1)S(1)} %get-tuple-element.30.pack_a), channel_id=1, source_target_pairs={{0,1},{1,0},{2,3},{3,2},{4,5},{5,4},{6,7},{7,6},{8,9},{9,8},{10,11... | collective-permute-start | bytes 454664 | tf_op jit(solution)/shard_map/ppermute | solution.py:346
